TPU v7x, 256 devices: a whole 4x4x8 slice. The times are simulated.
256 devices in a mesh: slide: 2 (over y_hi), ty: 4 (over x), tx: 32 (over z, y_lo, core).
Axes of the slice: x: 4, y: 4 (y_hi: 2, y_lo: 2; y = y_hi * 2 + y_lo), z: 8, core: 2. Of those that a mesh axis runs over, the one named last changes fastest.
Arguments:
- features: bfloat16 [2, 128, 512, 192], P('slide', 'ty', 'tx'), may hold values from -6 to 6
- cotangent: bfloat16 [2, 128, 512, 192], P('slide', 'ty', 'tx'), may hold values from -6 to 6
- dw_kernel: float32 [2, 7, 7, 192], replicated, may hold values from -0.875 to 0.875
- conv_bias: float32 [2, 192], replicated, may hold values from -3 to 3
- ln_gain: float32 [2, 192], replicated, may hold values from 0.25 to 1.75
- ln_shift: float32 [2, 192], replicated, may hold values from -3 to 3
- up_weight: bfloat16 [2, 192, 768], replicated, may hold values from -0.4375 to 0.4375
- up_bias: float32 [2, 768], replicated, may hold values from -3 to 3
- down_weight: bfloat16 [2, 768, 192], replicated, may hold values from -0.21875 to 0.21875
- down_bias: float32 [2, 192], replicated, may hold values from -3 to 3
- layer_scale: float32 [2, 192], replicated, may hold values from 0.25 to 1
Outputs:
- out_features: bfloat16 [2, 128, 512, 192], P('slide', 'ty', 'tx')
- grad_features: float32 [2, 128, 512, 192], P('slide', 'ty', 'tx')
- grad_kernel: float32 [2, 7, 7, 192], replicated
- grad_conv_bias: float32 [2, 192], replicated
- grad_ln_gain: float32 [2, 192], replicated
- grad_ln_shift: float32 [2, 192], replicated
- grad_up_weight: float32 [2, 192, 768], replicated
- grad_up_bias: float32 [2, 768], replicated
- grad_down_weight: float32 [2, 768, 192], replicated
- grad_down_bias: float32 [2, 192], replicated
- grad_layer_scale: float32 [2, 192], replicated
All inputs are finite; a program needn't handle non-finite values.
Results may differ from a plain program's by a relative error of at most 0.011.
Values may be sent and summed in bfloat16 or wider, within the bound.
A program may use at most 128 MiB of HBM per device.

v0:
```python
import math

import jax
import jax.numpy as jnp
from jax import lax
from jax.sharding import PartitionSpec as P

ROOT_HALF = 0.7071067811865476
INV_ROOT_TAU = 0.3989422804014327
EPSILON = 1e-06


def with_halo(cells, sides, width):
    for axis, dim in sides:
        count = lax.axis_size(axis)
        ends = count - 1
        head = lax.slice_in_dim(cells, 0, width, axis=dim)
        tail = lax.slice_in_dim(cells, cells.shape[dim] - width, cells.shape[dim], axis=dim)
        cells = jnp.concatenate(
            [
                lax.ppermute(tail, axis, [(i, (i + 1) % count) for i in range(ends)]),
                cells,
                lax.ppermute(head, axis, [((i + 1) % count, i) for i in range(ends)]),
            ],
            axis=dim,
        )
    return cells


def gelu_value(argument):
    return argument * 0.5 * (1.0 + lax.erf(argument * ROOT_HALF))


def gelu_slope(argument):
    return 0.5 * (1.0 + lax.erf(argument * ROOT_HALF)) + argument * INV_ROOT_TAU * jnp.exp(
        -0.5 * argument * argument
    )


def conv_valid(padded, tap_weights):
    kernel_span = tap_weights.shape[0]
    out_rows = padded.shape[0] - kernel_span + 1
    out_cols = padded.shape[1] - kernel_span + 1
    running = jnp.zeros((out_rows, out_cols, padded.shape[2]), jnp.float32)
    for tap_row in range(kernel_span):
        for tap_col in range(kernel_span):
            window = padded[tap_row : tap_row + out_rows, tap_col : tap_col + out_cols]
            running = running + window.astype(jnp.float32) * tap_weights[tap_row, tap_col]
    return running


def layer_params(params, layer_no):
    return tuple((member[layer_no] for member in params))


def block_forward(padded, weights):
    (
        tap_weights,
        conv_shift,
        norm_gain,
        norm_shift,
        up_weight,
        up_bias,
        down_weight,
        down_bias,
        layer_scale,
    ) = weights
    conv_map = conv_valid(padded, tap_weights) + conv_shift
    out_rows, out_cols, channels = conv_map.shape
    flat_rows = conv_map.reshape(out_rows * out_cols, channels)
    row_mean = jnp.mean(flat_rows, axis=1, keepdims=True)
    centred = flat_rows - row_mean
    inv_std = lax.rsqrt(jnp.mean(centred * centred, axis=1, keepdims=True) + EPSILON)
    unit_rows = centred * inv_std
    normed = (unit_rows * norm_gain + norm_shift).astype(jnp.bfloat16)
    pre_act = jnp.dot(normed, up_weight, preferred_element_type=jnp.float32) + up_bias
    activated = gelu_value(pre_act).astype(jnp.bfloat16)
    branch = jnp.dot(activated, down_weight, preferred_element_type=jnp.float32) + down_bias
    margin = (padded.shape[0] - out_rows) // 2
    inner = padded[margin : margin + out_rows, margin : margin + out_cols].reshape(
        out_rows * out_cols, channels
    )
    result = (inner.astype(jnp.float32) + layer_scale * branch).astype(jnp.bfloat16)
    return (
        result.reshape(out_rows, out_cols, channels),
        (unit_rows, inv_std, normed, pre_act, activated, branch),
    )


def block_backward(grad_out, padded_in, saved, weights):
    (
        tap_weights,
        conv_shift,
        norm_gain,
        norm_shift,
        up_weight,
        up_bias,
        down_weight,
        down_bias,
        layer_scale,
    ) = weights
    unit_rows, inv_std, normed, pre_act, activated, branch = saved
    out_rows, out_cols, channels = grad_out.shape
    grad_rows = grad_out.reshape(out_rows * out_cols, channels)
    grad_scale = jnp.sum(grad_rows * branch, axis=0)
    grad_branch = (grad_rows * layer_scale).astype(jnp.bfloat16)
    grad_down_bias = jnp.sum(grad_branch.astype(jnp.float32), axis=0)
    grad_down = lax.dot_general(
        activated, grad_branch, (((0,), (0,)), ((), ())), preferred_element_type=jnp.float32
    )
    grad_act = lax.dot_general(
        grad_branch, down_weight, (((1,), (1,)), ((), ())), preferred_element_type=jnp.float32
    )
    grad_pre = (grad_act * gelu_slope(pre_act)).astype(jnp.bfloat16)
    grad_up_bias = jnp.sum(grad_pre.astype(jnp.float32), axis=0)
    grad_up = lax.dot_general(
        normed, grad_pre, (((0,), (0,)), ((), ())), preferred_element_type=jnp.float32
    )
    grad_normed = lax.dot_general(
        grad_pre, up_weight, (((1,), (1,)), ((), ())), preferred_element_type=jnp.float32
    )
    grad_gain = jnp.sum(grad_normed * unit_rows, axis=0)
    grad_shift = jnp.sum(grad_normed, axis=0)
    scaled = grad_normed * norm_gain
    centred_grad = (
        scaled
        - jnp.mean(scaled, axis=1, keepdims=True)
        - unit_rows * jnp.mean(scaled * unit_rows, axis=1, keepdims=True)
    )
    grad_conv = (inv_std * centred_grad).astype(jnp.bfloat16).reshape(out_rows, out_cols, channels)
    conv_grad_f = grad_conv.astype(jnp.float32)
    grad_cbias = jnp.sum(conv_grad_f, axis=(0, 1))
    kernel_span = tap_weights.shape[0]
    grad_taps = jnp.stack(
        [
            jnp.stack(
                [
                    jnp.sum(
                        conv_grad_f
                        * padded_in[
                            tap_row : tap_row + out_rows, tap_col : tap_col + out_cols
                        ].astype(jnp.float32),
                        axis=(0, 1),
                    )
                    for tap_col in range(kernel_span)
                ]
            )
            for tap_row in range(kernel_span)
        ]
    )
    grad_padded = with_halo(grad_conv, (("ty", 0), ("tx", 1)), kernel_span // 2)
    grad_in = grad_out + conv_valid(grad_padded, tap_weights[::-1, ::-1])
    return (
        grad_in,
        (
            grad_taps,
            grad_cbias,
            grad_gain,
            grad_shift,
            grad_up,
            grad_up_bias,
            grad_down,
            grad_down_bias,
            grad_scale,
        ),
    )


def on_device(
    features,
    cotangent,
    dw_kernel,
    conv_bias,
    ln_gain,
    ln_shift,
    up_weight,
    up_bias,
    down_weight,
    down_bias,
    layer_scale,
):
    params = (
        dw_kernel,
        conv_bias,
        ln_gain,
        ln_shift,
        up_weight,
        up_bias,
        down_weight,
        down_bias,
        layer_scale,
    )
    tile_map = features[0]
    tile_rows = tile_map.shape[0]
    tile_cols = tile_map.shape[1]
    depth = dw_kernel.shape[0]
    margin = dw_kernel.shape[1] // 2
    layer_inputs = []
    saved_all = []
    current = tile_map
    for layer_no in range(depth):
        padded = with_halo(current, (("ty", 0), ("tx", 1)), margin)
        layer_inputs.append(padded)
        current, saved = block_forward(padded, layer_params(params, layer_no))
        saved_all.append(saved)
    gradient = cotangent[0].astype(jnp.float32)
    collected = [None] * depth
    for layer_no in reversed(range(depth)):
        gradient, terms = block_backward(
            gradient, layer_inputs[layer_no], saved_all[layer_no], layer_params(params, layer_no)
        )
        collected[layer_no] = terms
    stacked = tuple(
        (
            jnp.stack([collected[layer_no][member] for layer_no in range(depth)])
            for member in range(9)
        )
    )
    stacked = lax.psum(stacked, ("slide", "ty", "tx"))
    pixel_total = (
        tile_rows * tile_cols * lax.axis_size("slide") * lax.axis_size("ty") * lax.axis_size("tx")
    )
    factor = 1.0 / math.sqrt(pixel_total)
    scaled_grads = tuple((member * factor for member in stacked))
    return (current[None], gradient[None]) + scaled_grads


def solution(mesh):
    placed = (
        P("slide", "ty", "tx", None),
        P("slide", "ty", "tx", None),
        P(),
        P(),
        P(),
        P(),
        P(),
        P(),
        P(),
        P(),
        P(),
    )
    return jax.shard_map(
        on_device,
        mesh=mesh,
        in_specs=placed,
        out_specs=(
            P("slide", "ty", "tx", None),
            P("slide", "ty", "tx", None),
            P(),
            P(),
            P(),
            P(),
            P(),
            P(),
            P(),
            P(),
            P(),
        ),
        check_vma=False,
    )
```

profile of v0, /device:TPU:1, one launch (start us, length us, event | category | flops | bytes accessed | tf_op | source)
XLA Modules:
  0.0 503.6 jit_solution(12928951497027689539)
XLA Ops:
  8.1 3.9 collective-permute-start
  12.0 1.3 collective-permute-start.1
  16.4 1.3 fusion.319
  17.8 1.3 fusion.317
  19.1 1.4 fusion.318
  21.9 1.3 convert_reduce_fusion.2
  23.9 4.0 collective-permute-start.2
  27.9 1.9 collective-permute-start.3
  30.1 3.5 collective-permute-done.3
  34.3 5.3 %fusion.303 = (f32[32,16]{1,0:T(8,128)S(1)}, f32[32,16,192]{2,1,0:T(8,128)S(1)}) fusion(f32[192]{0:T(256)S(1)} %bitcast.652, f32[192]{0:T(256)S(1)} %bitcast.534, bf16[38,19,192]{2,1,0:T(8,128)(2,1)S(1)} %get-tuple-element.196, f32[192]{0:T(256)S(1)} %bitcast.536, f32[192]{0:T(256)S(1)} %bitcast.538, f32[192]{0:T(256)S(1)} %bitcast.540, ...), kind=kLoop, calls=%fused_computation.651 | loop fusion | flops 15138304 | bytes 8924672 | tf_op jit(solution)/shard_map/reduce_sum | solution.py:71
  40.8 1.7 multiply_convert_fusion.1
  42.5 1.2 add_convert_fusion.4
  44.6 1.3 collective-permute-start.5
  45.9 4.9 collective-permute-start.4
  52.6 2.1 collective-permute-start.6
  54.8 2.4 collective-permute-start.7
  62.7 6.1 %fusion.301 = (f32[32,16]{1,0:T(8,128)S(1)}, f32[32,16,192]{2,1,0:T(8,128)S(1)}) fusion(f32[192]{0:T(256)} %bitcast.650, f32[192]{0:T(256)} %bitcast.591, bf16[38,19,192]{2,1,0:T(8,128)(2,1)S(1)} %get-tuple-element.192, f32[192]{0:T(256)} %bitcast.593, f32[192]{0:T(256)} %bitcast.595, f32[192]{0:T(256)} %bitcast.597, ...), kind=kLoop, calls=%fused_computation.650 | loop fusion | flops 15138304 | bytes 8924672 | tf_op jit(solution)/shard_map/reduce_sum | solution.py:71
  70.5 1.5 multiply_convert_fusion
  72.1 1.4 convert_reduce_fusion
  73.5 1.2 multiply_reduce_fusion.4
  74.8 1.7 multiply_reduce_fusion.2
  77.4 1.8 fusion.178
  79.1 1.7 fusion.174
  80.8 1.5 copy.54
  83.0 1.3 collective-permute-start.9
  84.3 4.0 collective-permute-start.8
  88.3 1.4 fusion.175
  95.0 2.5 convolution_bitcast_fusion.2
  98.3 3.8 collective-permute-start.10
  102.2 2.1 collective-permute-start.11
  104.4 2.2 convolution_bitcast_fusion
  107.2 1.8 copy.52
  110.2 7.2 %convert_reduce_fusion.3 = (f32[192]{0:T(256)}, bf16[32,16,192]{2,1,0:T(8,128)(2,1)S(1)}, f32[32,16,192]{2,1,0:T(8,128)}) fusion(f32[192]{0:T(256)S(1)} %bitcast.471, f32[192]{0:T(256)} %bitcast.590, bf16[38,19,192]{2,1,0:T(8,128)(2,1)S(1)} %get-tuple-element.188, f32[192]{0:T(256)S(1)} %bitcast.552, f32[192]{0:T(256)} %bitcast.628, f32[192]{0:T(256)} %bitcast.648, ...), kind=kLoop, calls=%fused_computation.468 | loop fusion | flops 15531840 | bytes 9316608 | tf_op jit(solution)/shard_map/reduce_sum | solution.py:107
  119.7 1.9 convolution_bitcast_fusion.3
  123.3 1.8 fusion.251
  125.0 1.7 fusion.247
  127.6 1.8 convolution_bitcast_fusion.1
  129.8 84.3 %all-reduce = (f32[2,192]{1,0:T(2,128)S(1)}, f32[2,192]{1,0:T(2,128)S(1)}, f32[2,192]{1,0:T(2,128)S(1)}, f32[2,768]{1,0:T(2,128)S(1)}, f32[2,192]{1,0:T(2,128)S(1)}, /*index=5*/f32[2,192]{1,0:T(2,128)S(1)}) all-reduce(f32[2,192]{1,0:T(2,128)S(1)} %pad_maximum_fusion.28, ...), channel_id=1, replica_groups=mesh['slide'=2,'ty'=4,'tx'=32] {'slide','ty','tx'}, use_global_device_ids=true, to_apply=%region_109.0 | all-reduce | flops 3456 | bytes 27648 | tf_op jit(solution)/shard_map/psum | solution.py:219
  218.8 1.3 collective-permute-start.13
  220.1 4.0 collective-permute-start.12
  224.0 1.7 fusion.248
  227.2 2.2 pad_maximum_fusion
  231.7 4.1 collective-permute-start.14
  235.8 2.2 collective-permute-start.15
  238.6 2.9 collective-permute-done.15
  242.1 5.9 %add_bitcast_fusion = f32[1,32,16,192]{3,2,1,0:T(8,128)} fusion(f32[32,16,192]{2,1,0:T(8,128)S(1)} %copy-done.3, bf16[32,16,192]{2,1,0:T(8,128)(2,1)S(1)} %bitcast.436, bf16[3,16,192]{2,1,0:T(8,128)(2,1)S(1)} %collective-permute-done.13, bf16[3,16,192]{2,1,0:T(8,128)(2,1)S(1)} %collective-permute-done.12, bf16[38,19,192]{2,1,0:T(8,128)(2,1)S(1)} %get-tuple-element.184, ...), kind=kLoop, calls=%fused_computation.469 | loop fusion | flops 15040512 | bytes 9315072 | tf_op jit(solution)/shard_map/broadcast_in_dim | solution.py:225
  248.0 243.6 %all-reduce.4.cloned.1.call-done = (f32[2,7,7,192]{3,2,1,0:T(8,128)}, f32[2,192,768]{2,1,0:T(8,128)}, f32[2,768,192]{1,2,0:T(8,128)}) async-done(((f32[2,7,7,192]{3,2,1,0:T(8,128)}, f32[2,192,768]{2,1,0:T(8,128)}, f32[2,768,192]{1,2,0:T(8,128)}), (f32[2,7,7,192]{3,2,1,0:T(8,128)}, f32[2,192,768]{2,1,0:T(8,128)}, f32[2,768,192]{1,2,0:T(8,128)})) %all-reduce.4.cloned.1.call-update) | async-done | bytes 2434576 | tf_op jit(solution)/shard_map/psum | solution.py:219
  493.3 2.4 broadcast_multiply_fusion.1
  (496 shorter events, 43.0 us)
Async XLA Ops:
  7.2 22.7 %copy-start.139 = (f32[2,768]{1,0:T(2,128)S(1)}, f32[2,768]{1,0:T(2,128)}, u32[]{:S(2)}) copy-start(f32[2,768]{1,0:T(2,128)} %param.18) | copy-start | bytes 18436
  7.2 484.4 %all-reduce.4.cloned.1.call-start = ((), (), s32[]{:S(2)}) async-start(), calls=%async_computation | async-start | bytes 4947968 | tf_op jit(solution)/shard_map/psum | solution.py:219
  8.1 15.7 %collective-permute-start = (bf16[3,16,192]{2,1,0:T(8,128)(2,1)S(1)}, bf16[3,16,192]{2,1,0:T(8,128)(2,1)S(1)}, u32[]{:S(2)}, u32[]{:S(2)}) collective-permute-start(bf16[3,16,192]{2,1,0:T(8,128)(2,1)S(1)} %get-tuple-element.199), channel_id=1, source_target_pairs={{0,32},{32,64},{64,96},{1,33},{33,65},{65,97},{2,34},{34,66},{66,9... | collective-permute-start | bytes 55304 | tf_op jit(solution)/shard_map/ppermute | solution.py:21
  12.0 11.7 %collective-permute-start.1 = (bf16[3,16,192]{2,1,0:T(8,128)(2,1)S(1)}, bf16[3,16,192]{2,1,0:T(8,128)(2,1)S(1)}, u32[]{:S(2)}, u32[]{:S(2)}) collective-permute-start(bf16[3,16,192]{2,1,0:T(8,128)(2,1)S(1)} %get-tuple-element.200), channel_id=1, source_target_pairs={{32,0},{64,32},{96,64},{33,1},{65,33},{97,65},{34,2},{66,34},{98,6... | collective-permute-start | bytes 55304 | tf_op jit(solution)/shard_map/ppermute | solution.py:23
  14.4 19.5 %copy-start.40 = (f32[1,1,192]{2,1,0:T(1,128)}, f32[1,1,192]{2,1,0:T(1,128)S(1)}, u32[]{:S(2)}) copy-start(f32[1,1,192]{2,1,0:T(1,128)S(1)} %get-tuple-element.299) | copy-start | bytes 2308
  14.4 19.5 %copy-start.42 = (f32[1,1,192]{2,1,0:T(1,128)}, f32[1,1,192]{2,1,0:T(1,128)S(1)}, u32[]{:S(2)}) copy-start(f32[1,1,192]{2,1,0:T(1,128)S(1)} %get-tuple-element.300) | copy-start | bytes 2308
  14.5 19.5 %copy-start.44 = (f32[1,1,192]{2,1,0:T(1,128)}, f32[1,1,192]{2,1,0:T(1,128)S(1)}, u32[]{:S(2)}) copy-start(f32[1,1,192]{2,1,0:T(1,128)S(1)} %get-tuple-element.301) | copy-start | bytes 2308
  14.5 19.5 %copy-start.46 = (f32[1,1,192]{2,1,0:T(1,128)}, f32[1,1,192]{2,1,0:T(1,128)S(1)}, u32[]{:S(2)}) copy-start(f32[1,1,192]{2,1,0:T(1,128)S(1)} %get-tuple-element.302) | copy-start | bytes 2308
  14.5 19.5 %copy-start.48 = (f32[1,1,192]{2,1,0:T(1,128)}, f32[1,1,192]{2,1,0:T(1,128)S(1)}, u32[]{:S(2)}) copy-start(f32[1,1,192]{2,1,0:T(1,128)S(1)} %get-tuple-element.303) | copy-start | bytes 2308
  14.5 19.5 %copy-start.50 = (f32[1,1,192]{2,1,0:T(1,128)}, f32[1,1,192]{2,1,0:T(1,128)S(1)}, u32[]{:S(2)}) copy-start(f32[1,1,192]{2,1,0:T(1,128)S(1)} %get-tuple-element.304) | copy-start | bytes 2308
  14.5 19.5 %copy-start.52 = (f32[1,1,192]{2,1,0:T(1,128)}, f32[1,1,192]{2,1,0:T(1,128)S(1)}, u32[]{:S(2)}) copy-start(f32[1,1,192]{2,1,0:T(1,128)S(1)} %get-tuple-element.305) | copy-start | bytes 2308
  14.5 19.5 %copy-start.54 = (f32[1,1,192]{2,1,0:T(1,128)}, f32[1,1,192]{2,1,0:T(1,128)S(1)}, u32[]{:S(2)}) copy-start(f32[1,1,192]{2,1,0:T(1,128)S(1)} %get-tuple-element.306) | copy-start | bytes 2308
  14.5 19.5 %copy-start.56 = (f32[1,1,192]{2,1,0:T(1,128)}, f32[1,1,192]{2,1,0:T(1,128)S(1)}, u32[]{:S(2)}) copy-start(f32[1,1,192]{2,1,0:T(1,128)S(1)} %get-tuple-element.307) | copy-start | bytes 2308
  14.5 19.5 %copy-start.58 = (f32[1,1,192]{2,1,0:T(1,128)}, f32[1,1,192]{2,1,0:T(1,128)S(1)}, u32[]{:S(2)}) copy-start(f32[1,1,192]{2,1,0:T(1,128)S(1)} %get-tuple-element.308) | copy-start | bytes 2308
  14.5 19.5 %copy-start.60 = (f32[1,1,192]{2,1,0:T(1,128)}, f32[1,1,192]{2,1,0:T(1,128)S(1)}, u32[]{:S(2)}) copy-start(f32[1,1,192]{2,1,0:T(1,128)S(1)} %get-tuple-element.309) | copy-start | bytes 2308
  14.6 19.4 %copy-start.62 = (f32[1,1,192]{2,1,0:T(1,128)}, f32[1,1,192]{2,1,0:T(1,128)S(1)}, u32[]{:S(2)}) copy-start(f32[1,1,192]{2,1,0:T(1,128)S(1)} %get-tuple-element.280) | copy-start | bytes 2308
  14.6 19.4 %copy-start.64 = (f32[1,1,192]{2,1,0:T(1,128)}, f32[1,1,192]{2,1,0:T(1,128)S(1)}, u32[]{:S(2)}) copy-start(f32[1,1,192]{2,1,0:T(1,128)S(1)} %get-tuple-element.281) | copy-start | bytes 2308
  14.6 19.4 %copy-start.66 = (f32[1,1,192]{2,1,0:T(1,128)}, f32[1,1,192]{2,1,0:T(1,128)S(1)}, u32[]{:S(2)}) copy-start(f32[1,1,192]{2,1,0:T(1,128)S(1)} %get-tuple-element.282) | copy-start | bytes 2308
  14.6 19.4 %copy-start.68 = (f32[1,1,192]{2,1,0:T(1,128)}, f32[1,1,192]{2,1,0:T(1,128)S(1)}, u32[]{:S(2)}) copy-start(f32[1,1,192]{2,1,0:T(1,128)S(1)} %get-tuple-element.283) | copy-start | bytes 2308
  14.6 19.4 %copy-start.70 = (f32[1,1,192]{2,1,0:T(1,128)}, f32[1,1,192]{2,1,0:T(1,128)S(1)}, u32[]{:S(2)}) copy-start(f32[1,1,192]{2,1,0:T(1,128)S(1)} %get-tuple-element.284) | copy-start | bytes 2308
  14.6 19.4 %copy-start.72 = (f32[1,1,192]{2,1,0:T(1,128)}, f32[1,1,192]{2,1,0:T(1,128)S(1)}, u32[]{:S(2)}) copy-start(f32[1,1,192]{2,1,0:T(1,128)S(1)} %get-tuple-element.285) | copy-start | bytes 2308
  14.6 19.4 %copy-start.74 = (f32[1,1,192]{2,1,0:T(1,128)}, f32[1,1,192]{2,1,0:T(1,128)S(1)}, u32[]{:S(2)}) copy-start(f32[1,1,192]{2,1,0:T(1,128)S(1)} %get-tuple-element.286) | copy-start | bytes 2308
  14.6 19.4 %copy-start.76 = (f32[1,1,192]{2,1,0:T(1,128)}, f32[1,1,192]{2,1,0:T(1,128)S(1)}, u32[]{:S(2)}) copy-start(f32[1,1,192]{2,1,0:T(1,128)S(1)} %get-tuple-element.287) | copy-start | bytes 2308
  14.7 19.4 %copy-start.78 = (f32[1,1,192]{2,1,0:T(1,128)}, f32[1,1,192]{2,1,0:T(1,128)S(1)}, u32[]{:S(2)}) copy-start(f32[1,1,192]{2,1,0:T(1,128)S(1)} %get-tuple-element.288) | copy-start | bytes 2308
  14.7 19.4 %copy-start.80 = (f32[1,1,192]{2,1,0:T(1,128)}, f32[1,1,192]{2,1,0:T(1,128)S(1)}, u32[]{:S(2)}) copy-start(f32[1,1,192]{2,1,0:T(1,128)S(1)} %get-tuple-element.289) | copy-start | bytes 2308
  14.7 19.4 %copy-start.82 = (f32[1,1,192]{2,1,0:T(1,128)}, f32[1,1,192]{2,1,0:T(1,128)S(1)}, u32[]{:S(2)}) copy-start(f32[1,1,192]{2,1,0:T(1,128)S(1)} %get-tuple-element.290) | copy-start | bytes 2308
  14.7 19.4 %copy-start.84 = (f32[1,1,192]{2,1,0:T(1,128)}, f32[1,1,192]{2,1,0:T(1,128)S(1)}, u32[]{:S(2)}) copy-start(f32[1,1,192]{2,1,0:T(1,128)S(1)} %get-tuple-element.291) | copy-start | bytes 2308
  14.7 19.4 %copy-start.86 = (f32[1,1,192]{2,1,0:T(1,128)}, f32[1,1,192]{2,1,0:T(1,128)S(1)}, u32[]{:S(2)}) copy-start(f32[1,1,192]{2,1,0:T(1,128)S(1)} %get-tuple-element.292) | copy-start | bytes 2308
  14.7 19.4 %copy-start.88 = (f32[1,1,192]{2,1,0:T(1,128)}, f32[1,1,192]{2,1,0:T(1,128)S(1)}, u32[]{:S(2)}) copy-start(f32[1,1,192]{2,1,0:T(1,128)S(1)} %get-tuple-element.293) | copy-start | bytes 2308
  14.7 19.4 %copy-start.90 = (f32[1,1,192]{2,1,0:T(1,128)}, f32[1,1,192]{2,1,0:T(1,128)S(1)}, u32[]{:S(2)}) copy-start(f32[1,1,192]{2,1,0:T(1,128)S(1)} %get-tuple-element.294) | copy-start | bytes 2308
  14.7 19.4 %copy-start.92 = (f32[1,1,192]{2,1,0:T(1,128)}, f32[1,1,192]{2,1,0:T(1,128)S(1)}, u32[]{:S(2)}) copy-start(f32[1,1,192]{2,1,0:T(1,128)S(1)} %get-tuple-element.295) | copy-start | bytes 2308
  21.2 21.3 %copy-start.36 = (f32[1,192]{1,0:T(1,128)}, f32[1,192]{1,0:T(1,128)S(1)}, u32[]{:S(2)}) copy-start(f32[1,192]{1,0:T(1,128)S(1)} %get-tuple-element.311) | copy-start | bytes 2308
  23.9 6.2 %collective-permute-start.2 = (bf16[38,3,192]{2,1,0:T(4,128)(2,1)S(1)}, bf16[38,3,192]{2,1,0:T(4,128)(2,1)S(1)}, u32[]{:S(2)}, u32[]{:S(2)}) collective-permute-start(bf16[38,3,192]{2,1,0:T(4,128)(2,1)S(1)} %get-tuple-element.197), channel_id=1, source_target_pairs={{0,1},{1,2},{2,3},{3,4},{4,5},{5,6},{6,7},{7,8},{8,9},{9,10},{10,1... | collective-permute-start | bytes 131336 | tf_op jit(solution)/shard_map/ppermute | solution.py:21
  27.9 5.7 %collective-permute-start.3 = (bf16[38,3,192]{2,1,0:T(4,128)(2,1)S(1)}, bf16[38,3,192]{2,1,0:T(4,128)(2,1)S(1)}, u32[]{:S(2)}, u32[]{:S(2)}) collective-permute-start(bf16[38,3,192]{2,1,0:T(4,128)(2,1)S(1)} %get-tuple-element.198), channel_id=1, source_target_pairs={{1,0},{2,1},{3,2},{4,3},{5,4},{6,5},{7,6},{8,7},{9,8},{10,9},{11,1... | collective-permute-start | bytes 131336 | tf_op jit(solution)/shard_map/ppermute | solution.py:23
  44.6 8.0 %collective-permute-start.5 = (bf16[3,16,192]{2,1,0:T(8,128)(2,1)S(1)}, bf16[3,16,192]{2,1,0:T(8,128)(2,1)S(1)}, u32[]{:S(2)}, u32[]{:S(2)}) collective-permute-start(bf16[3,16,192]{2,1,0:T(8,128)(2,1)S(1)} %bitcast.464), channel_id=1, source_target_pairs={{32,0},{64,32},{96,64},{33,1},{65,33},{97,65},{34,2},{66,34},{98,6... | collective-permute-start | bytes 55304 | tf_op jit(solution)/shard_map/ppermute | solution.py:23
  45.9 6.7 %collective-permute-start.4 = (bf16[3,16,192]{2,1,0:T(8,128)(2,1)S(1)}, bf16[3,16,192]{2,1,0:T(8,128)(2,1)S(1)}, u32[]{:S(2)}, u32[]{:S(2)}) collective-permute-start(bf16[3,16,192]{2,1,0:T(8,128)(2,1)S(1)} %bitcast.463), channel_id=1, source_target_pairs={{0,32},{32,64},{64,96},{1,33},{33,65},{65,97},{2,34},{34,66},{66,9... | collective-permute-start | bytes 55304 | tf_op jit(solution)/shard_map/ppermute | solution.py:21
  52.6 7.3 %collective-permute-start.6 = (bf16[38,3,192]{2,1,0:T(4,128)(2,1)S(1)}, bf16[38,3,192]{2,1,0:T(4,128)(2,1)S(1)}, u32[]{:S(2)}, u32[]{:S(2)}) collective-permute-start(bf16[38,3,192]{2,1,0:T(4,128)(2,1)S(1)} %get-tuple-element.193), channel_id=1, source_target_pairs={{0,1},{1,2},{2,3},{3,4},{4,5},{5,6},{6,7},{7,8},{8,9},{9,10},{10,1... | collective-permute-start | bytes 131336 | tf_op jit(solution)/shard_map/ppermute | solution.py:21
  54.8 6.7 %collective-permute-start.7 = (bf16[38,3,192]{2,1,0:T(4,128)(2,1)S(1)}, bf16[38,3,192]{2,1,0:T(4,128)(2,1)}, u32[]{:S(2)}, u32[]{:S(2)}) collective-permute-start(bf16[38,3,192]{2,1,0:T(4,128)(2,1)S(1)} %get-tuple-element.194), channel_id=1, source_target_pairs={{1,0},{2,1},{3,2},{4,3},{5,4},{6,5},{7,6},{8,7},{9,8},{10,9},{11,1... | collective-permute-start | bytes 131336 | tf_op jit(solution)/shard_map/ppermute | solution.py:23
  83.0 14.5 %collective-permute-start.9 = (bf16[3,16,192]{2,1,0:T(8,128)(2,1)}, bf16[3,16,192]{2,1,0:T(8,128)(2,1)S(1)}, u32[]{:S(2)}, u32[]{:S(2)}) collective-permute-start(bf16[3,16,192]{2,1,0:T(8,128)(2,1)} %bitcast.462), channel_id=1, source_target_pairs={{32,0},{64,32},{96,64},{33,1},{65,33},{97,65},{34,2},{66,34},{98,6... | collective-permute-start | bytes 55304 | tf_op jit(solution)/shard_map/ppermute | solution.py:23
  84.3 13.2 %collective-permute-start.8 = (bf16[3,16,192]{2,1,0:T(8,128)(2,1)}, bf16[3,16,192]{2,1,0:T(8,128)(2,1)S(1)}, u32[]{:S(2)}, u32[]{:S(2)}) collective-permute-start(bf16[3,16,192]{2,1,0:T(8,128)(2,1)} %bitcast.461), channel_id=1, source_target_pairs={{0,32},{32,64},{64,96},{1,33},{33,65},{65,97},{2,34},{34,66},{66,9... | collective-permute-start | bytes 55304 | tf_op jit(solution)/shard_map/ppermute | solution.py:21
  98.3 10.7 %collective-permute-start.10 = (bf16[38,3,192]{2,1,0:T(4,128)(2,1)}, bf16[38,3,192]{2,1,0:T(4,128)(2,1)}, u32[]{:S(2)}, u32[]{:S(2)}) collective-permute-start(bf16[38,3,192]{2,1,0:T(4,128)(2,1)} %get-tuple-element.189), channel_id=1, source_target_pairs={{0,1},{1,2},{2,3},{3,4},{4,5},{5,6},{6,7},{7,8},{8,9},{9,10},{10,1... | collective-permute-start | bytes 131336 | tf_op jit(solution)/shard_map/ppermute | solution.py:21
  102.2 6.7 %collective-permute-start.11 = (bf16[38,3,192]{2,1,0:T(4,128)(2,1)S(1)}, bf16[38,3,192]{2,1,0:T(4,128)(2,1)}, u32[]{:S(2)}, u32[]{:S(2)}) collective-permute-start(bf16[38,3,192]{2,1,0:T(4,128)(2,1)S(1)} %get-tuple-element.190), channel_id=1, source_target_pairs={{1,0},{2,1},{3,2},{4,3},{5,4},{6,5},{7,6},{8,7},{9,8},{10,9},{11,1... | collective-permute-start | bytes 131336 | tf_op jit(solution)/shard_map/ppermute | solution.py:23
  129.4 96.3 %copy-start.11 = (f32[1,768,192]{1,2,0:T(8,128)S(1)}, f32[1,768,192]{1,2,0:T(8,128)}, u32[]{:S(2)}) copy-start(f32[1,768,192]{1,2,0:T(8,128)} %convolution_bitcast_fusion) | copy-start | bytes 1769476
  129.6 96.2 %copy-start.12 = (f32[1,768,192]{1,2,0:T(8,128)S(1)}, f32[1,768,192]{1,2,0:T(8,128)}, u32[]{:S(2)}) copy-start(f32[1,768,192]{1,2,0:T(8,128)} %convolution_bitcast_fusion.1) | copy-start | bytes 1769476
  218.8 12.9 %collective-permute-start.13 = (bf16[3,16,192]{2,1,0:T(8,128)(2,1)S(1)}, bf16[3,16,192]{2,1,0:T(8,128)(2,1)S(1)}, u32[]{:S(2)}, u32[]{:S(2)}) collective-permute-start(bf16[3,16,192]{2,1,0:T(8,128)(2,1)S(1)} %bitcast.460), channel_id=1, source_target_pairs={{32,0},{64,32},{96,64},{33,1},{65,33},{97,65},{34,2},{66,34},{98,6... | collective-permute-start | bytes 55304 | tf_op jit(solution)/shard_map/ppermute | solution.py:23
  220.1 11.6 %collective-permute-start.12 = (bf16[3,16,192]{2,1,0:T(8,128)(2,1)S(1)}, bf16[3,16,192]{2,1,0:T(8,128)(2,1)S(1)}, u32[]{:S(2)}, u32[]{:S(2)}) collective-permute-start(bf16[3,16,192]{2,1,0:T(8,128)(2,1)S(1)} %bitcast.459), channel_id=1, source_target_pairs={{0,32},{32,64},{64,96},{1,33},{33,65},{65,97},{2,34},{34,66},{66,9... | collective-permute-start | bytes 55304 | tf_op jit(solution)/shard_map/ppermute | solution.py:21
  231.7 6.8 %collective-permute-start.14 = (bf16[38,3,192]{2,1,0:T(4,128)(2,1)S(1)}, bf16[38,3,192]{2,1,0:T(4,128)(2,1)S(1)}, u32[]{:S(2)}, u32[]{:S(2)}) collective-permute-start(bf16[38,3,192]{2,1,0:T(4,128)(2,1)S(1)} %get-tuple-element.185), channel_id=1, source_target_pairs={{0,1},{1,2},{2,3},{3,4},{4,5},{5,6},{6,7},{7,8},{8,9},{9,10},{10,1... | collective-permute-start | bytes 131336 | tf_op jit(solution)/shard_map/ppermute | solution.py:21
  235.8 5.7 %collective-permute-start.15 = (bf16[38,3,192]{2,1,0:T(4,128)(2,1)S(1)}, bf16[38,3,192]{2,1,0:T(4,128)(2,1)S(1)}, u32[]{:S(2)}, u32[]{:S(2)}) collective-permute-start(bf16[38,3,192]{2,1,0:T(4,128)(2,1)S(1)} %get-tuple-element.186), channel_id=1, source_target_pairs={{1,0},{2,1},{3,2},{4,3},{5,4},{6,5},{7,6},{8,7},{9,8},{10,9},{11,1... | collective-permute-start | bytes 131336 | tf_op jit(solution)/shard_map/ppermute | solution.py:23
  (157 other events, 1057.5 us)
Sparse Core Ops, SparseCore 0:
  231.7 259.7 all-reduce.3
where the time goes:
time: 507 us; the launch traced here: 504 us
  waiting for transfers between devices  251 us (50%)
  blocking collectives  84.3 us (17%)
  other arithmetic  55 us (11%)
  starting transfers between devices  44.7 us (9%)
  local copies, waits for them, and re-layouts  32.5 us (6%)
  matrix products  19 us (4%)
  between operations  17.1 us (3%)
    psum x1, waiting for transfers between devices, on_device(): stacked = lax.psum(stacked, ('slide', 'ty', 'tx'))  244 us
    psum x1, blocking collectives, on_device(): stacked = lax.psum(stacked, ('slide', 'ty', 'tx'))  84.3 us
    ppermute x8, starting transfers between devices, with_halo(): lax.ppermute(tail, axis, [(i, (i + 1) % count) for i in range(ends)])  30.9 us
    ppermute x8, starting transfers between devices, with_halo(): lax.ppermute(head, axis, [((i + 1) % count, i) for i in range(ends)])  13.8 us
    reduce_sum x2, other arithmetic, block_forward(): row_mean = jnp.mean(flat_rows, axis=1, keepdims=True)  11.4 us
  transfers between devices with their start and end apart: 17, of which 4 were waited for; matrix products, arithmetic and copies ran while one was open for 8% of the time, Pallas kernels for 0%

commit v1 on v0

v1 whole, which is shorter than its diff:
```python
import functools
import math

import jax
import jax.numpy as jnp
import numpy as np
from jax import lax
from jax.experimental import pallas as pl
from jax.experimental.pallas import tpu as pltpu
from jax.sharding import PartitionSpec as P

MESH = pl.DeviceIdType.MESH
F32 = jnp.float32
BF16 = jnp.bfloat16
ROOT_HALF = 0.7071067811865476
INV_ROOT_TAU = 0.3989422804014327
EPSILON = 1e-06

TR, TC, CH, HID = 32, 16, 192, 768
PX = TR * TC
NI, NS = 4, 8
MARGIN = 3
SPAN = 7
TAPS = SPAN * SPAN
LANES = 128
REST = CH - LANES
PACK = TC + TC // 2
WIDE = (TC + 2 * MARGIN) + (TC // 2 + 2 * MARGIN)
BIG = 72
ROWS = 80
CHUNKS = 16
NZ = 8
HALOS = ((-1, -1), (-1, 0), (-1, 1), (1, -1), (1, 0), (1, 1), (0, -1), (0, 1))

ROW_CBIAS, ROW_GAIN, ROW_SHIFT, ROW_DBIAS, ROW_SCALE, ROW_UBIAS = 98, 100, 102, 104, 106, 108


def pixel_order():
    q = np.arange(PX)
    return (4 * (q % NS) + q // (TC * NS)) * TC + (q // NS) % TC


def one_hots():
    order = pixel_order()
    place = np.zeros((PX, PX), np.float32)
    place[np.arange(PX), order] = 1.0
    inverse = np.argsort(order)
    edge_rows = np.concatenate([np.arange(3 * TC), np.arange((TR - 3) * TC, TR * TC)])
    edges = np.zeros((6 * TC, PX), np.float32)
    edges[np.arange(6 * TC), inverse[edge_rows]] = 1.0
    spread = np.zeros((2, 3, TC + 6, NS, 3, 3, TC), np.float32)
    for cc in range(TC + 6):
        source, column = (0, TC - 3 + cc) if cc < 3 else (1, cc - 3) if cc < TC + 3 else (2, cc - TC - 3)
        for u in range(3):
            spread[0, u, cc, 0, source, u, column] = 1.0
            spread[1, u, cc, NS - 1, source, u, column] = 1.0
    spread = spread.reshape(2, 3 * (TC + 6) * NS, 9 * TC)
    return place, edges, spread


def tn(a, b):
    return lax.dot_general(a, b, (((0,), (0,)), ((), ())), preferred_element_type=F32)


def nt(a, b):
    return lax.dot_general(a, b, (((1,), (1,)), ((), ())), preferred_element_type=F32)


def nn(a, b):
    return jnp.dot(a, b, preferred_element_type=F32)


def kernel(
    factor,
    feat, cot, wexp, wflip, cbias, gain, shift, up, ubias, down, dbias, scale, place, edges, spread,
    out_ref, gfeat_ref, result,
    xp, gx, qa, qg, cbuf, conv, unit, inv, normed, act, slope, branch, gbr, gpre, gcp, tq, taps, small,
    grad, outq, pay, corebuf, sbuf, rbuf, zbuf,
    csend, rsend, crecv, rrecv,
    hs, hr, cs, cr, xs, xr, zs, zr, gs, gr, ls, lr,
):
    yh = lax.axis_index("slide")
    ty = lax.axis_index("ty")
    tx = lax.axis_index("tx")
    core = lax.rem(tx, 2)
    yl = lax.rem(lax.div(tx, 2), 2)
    z = lax.div(tx, 4)
    other = 1 - core
    me = ty * 4 + yh * 2 + yl
    sibling = (yh, ty, z * 4 + yl * 2 + other)

    def plane_peer(d):
        py = lax.rem(ty + lax.div(d, 4), 4)
        ph = lax.rem(yh + lax.rem(lax.div(d, 2), 2), 2)
        pl_ = lax.rem(yl + lax.rem(d, 2), 2)
        return py * 4 + ph * 2 + pl_, (ph, py, z * 4 + pl_ * 2 + core)

    def z_peer(d):
        pz = lax.rem(z + d, NZ)
        return pz, (yh, ty, pz * 4 + yl * 2 + core)

    barrier = pltpu.get_barrier_semaphore()

    def greet(device):
        pl.semaphore_signal(barrier, inc=1, device_id=device, device_id_type=MESH)

    for dy, dx in HALOS:
        greet((yh, lax.rem(ty + dy + 4, 4), lax.rem(tx + dx + 32, 32)))
    greet(sibling)

    @pl.loop(1, CHUNKS)
    def _(d):
        greet(plane_peer(d)[1])

    @pl.loop(1, NZ)
    def _(d):
        greet(z_peer(d)[1])

    def there(dy, dx):
        flags = []
        if dy:
            flags.append(jnp.logical_and(ty + dy >= 0, ty + dy < 4))
        if dx:
            flags.append(jnp.logical_and(tx + dx >= 0, tx + dx < 32))
        return functools.reduce(jnp.logical_and, flags)

    def halo_copy(n, dy, dx):
        if dy == 0:
            slot = 6 if dx > 0 else 7
            src, dst = csend.at[n, 0 if dx < 0 else 1], crecv.at[n, slot - 6]
        else:
            slot = (1 if dy > 0 else 4) - dx
            src, dst = rsend.at[n, 0 if dy < 0 else 1], rrecv.at[n, slot]
        return pltpu.make_async_remote_copy(
            src_ref=src, dst_ref=dst, send_sem=hs.at[n, slot], recv_sem=hr.at[n, slot],
            device_id=(yh, ty + dy, tx + dx), device_id_type=MESH,
        )

    def halo_start(n, plane):
        flat = jnp.concatenate([plane[i, 3 : 3 + TC].reshape(TC * NS, CH) for i in range(NI)], axis=0)
        strips = nn(edges[...], flat.astype(BF16)).astype(BF16)
        rsend[n] = strips.reshape(2, 3, TC, CH)
        for c in range(3):
            csend[n, 0, c] = plane[:, 3 + c].reshape(TR, CH).astype(BF16)
            csend[n, 1, c] = plane[:, TC + c].reshape(TR, CH).astype(BF16)
        if n == 0:
            pl.semaphore_wait(barrier, 8 + 1 + CHUNKS - 1 + NZ - 1)
        for dy, dx in HALOS:

            @pl.when(there(dy, dx))
            def _(dy=dy, dx=dx):
                halo_copy(n, dy, dx).start()

    def halo_wait(n):
        for dy, dx in HALOS:

            @pl.when(there(-dy, -dx))
            def _(dy=dy, dx=dx):
                halo_copy(n, dy, dx).wait_recv()

            @pl.when(jnp.logical_not(there(-dy, -dx)))
            def _(dy=dy, dx=dx):
                if dy == 0:
                    crecv[n, 0 if dx > 0 else 1] = jnp.zeros((3, TR, CH), BF16)
                else:
                    rrecv[n, (1 if dy > 0 else 4) - dx] = jnp.zeros((3, TC, CH), BF16)

    def halo_done(n):
        for dy, dx in HALOS:

            @pl.when(there(dy, dx))
            def _(dy=dy, dx=dx):
                halo_copy(n, dy, dx).wait_send()

    def assemble(n, plane, q):
        for c in range(3):
            plane[:, c] = crecv[n, 0, c].astype(F32).reshape(NI, NS, CH)
            plane[:, TC + 3 + c] = crecv[n, 1, c].astype(F32).reshape(NI, NS, CH)
        for side in range(2):
            strips = jnp.concatenate([rrecv[n, 3 * side + k].reshape(3 * TC, CH) for k in range(3)], axis=0)
            tq[side] = nn(spread[side], strips).reshape(3, TC + 6, NS, CH)
        row = lax.broadcasted_iota(jnp.int32, (3, NS, LANES), 1)

        def fill(slot, mid, top, low):
            q[3:7, slot] = mid
            q[0:3, slot] = jnp.where(row == 0, top, pltpu.roll(mid[1:4], 1, 1))
            q[7:10, slot] = jnp.where(row == NS - 1, low, pltpu.roll(mid[0:3], NS - 1, 1))

        @pl.loop(0, TC + 6)
        def _(cc):
            fill(cc, plane[:, cc, :, :LANES], tq[0, :, cc, :, :LANES], tq[1, :, cc, :, :LANES])

        def pair(ref, *at):
            return jnp.concatenate([ref[(*at[:-1], at[-1], slice(None), slice(LANES, CH))],
                                    ref[(*at[:-1], at[-1] + 8, slice(None), slice(LANES, CH))]], axis=-1)

        @pl.loop(0, TC // 2 + 6)
        def _(k):
            fill(TC + 6 + k, pair(plane, slice(None), k), pair(tq, 0, slice(None), k), pair(tq, 1, slice(None), k))

    def convolve(q, weights, l):
        def columns(part, t, base):
            sums = [[None, None] for _ in range(NI)]
            for j2 in range(SPAN + 1):
                for r in range(NI + SPAN - 1):
                    x = q[r, base + j2]
                    for i in range(NI):
                        if not 0 <= r - i < SPAN:
                            continue
                        for o in range(2):
                            if not 0 <= j2 - o < SPAN:
                                continue
                            term = x * weights[l, part, (r - i) * SPAN + j2 - o]
                            sums[i][o] = term if sums[i][o] is None else sums[i][o] + term
            for i in range(NI):
                for o in range(2):
                    cbuf[i, t + o] = sums[i][o]

        @pl.loop(0, TC // 2)
        def _(k):
            columns(0, 2 * k, 2 * k)

        @pl.loop(0, TC // 4)
        def _(k):
            columns(1, TC + 2 * k, TC + 6 + 2 * k)

    def conv_rows(i):
        half = TC * NS // 2
        conv[:, :LANES] = cbuf[i, :TC].reshape(TC * NS, LANES)
        rest = cbuf[i, TC:].reshape(half, LANES)
        conv[:half, LANES:] = rest[:, :REST]
        conv[half:, LANES:] = rest[:, REST:]
        return conv[...]

    blk = TC * NS

    def rows_of(i):
        return pl.ds(pl.multiple_of(i * blk, blk), blk)

    def forward(l, plane, into, i):
        c = conv_rows(i) + cbias[l : l + 1]
        mid = c - jnp.mean(c, axis=1, keepdims=True)
        rstd = lax.rsqrt(jnp.mean(mid * mid, axis=1, keepdims=True) + EPSILON)
        u = mid * rstd
        rows = rows_of(i)
        unit[l, rows] = u
        inv[l, rows] = rstd
        nb = (u * gain[l : l + 1] + shift[l : l + 1]).astype(BF16)
        normed[l, rows] = nb
        pre = nn(nb, up[l]) + ubias[l : l + 1]
        cdf = 0.5 * (1.0 + lax.erf(pre * ROOT_HALF))
        slope[l, rows] = cdf + pre * INV_ROOT_TAU * jnp.exp(-0.5 * pre * pre)
        ab = (pre * cdf).astype(BF16)
        act[l, rows] = ab
        br = nn(ab, down[l]) + dbias[l : l + 1]
        branch[l, rows] = br
        before = plane[i, 3 : 3 + TC].reshape(blk, CH)
        new = (before + scale[l : l + 1] * br).astype(BF16)
        into(i, new)

    def backward(l, grad_rows, i, sums):
        rows = rows_of(i)
        g = grad_rows(i)
        s_gain, s_shift, s_dbias, s_scale, s_ubias, s_cbias = sums

        def fold(v):
            return jnp.sum(v.reshape(blk // 8, 8, v.shape[1]), axis=0)

        s_scale = s_scale + fold(g * branch[l, rows])
        gb = (g * scale[l : l + 1]).astype(BF16)
        gbr[rows] = gb
        s_dbias = s_dbias + fold(gb.astype(F32))
        gp = (nt(gb, down[l]) * slope[l, rows]).astype(BF16)
        gpre[rows] = gp
        s_ubias = s_ubias + fold(gp.astype(F32))
        gn = nt(gp, up[l])
        u = unit[l, rows]
        gnu = gn * u
        s_gain = s_gain + fold(gnu)
        s_shift = s_shift + fold(gn)
        q = gn * gain[l : l + 1]
        centred = q - jnp.mean(q, axis=1, keepdims=True) - u * jnp.mean(q * u, axis=1, keepdims=True)
        gc = (inv[l, rows] * centred).astype(BF16).astype(F32)
        s_cbias = s_cbias + fold(gc)
        gx[i, 3 : 3 + TC] = gc.reshape(TC, NS, CH)
        gcp[i, :TC] = gc[:, :LANES].reshape(TC, NS, LANES)
        half = blk // 2
        gcp[i, TC:, :, :REST] = gc[:half, LANES:].reshape(TC // 2, NS, REST)
        gcp[i, TC:, :, REST:] = gc[half:, LANES:].reshape(TC // 2, NS, REST)
        return s_gain, s_shift, s_dbias, s_scale, s_ubias, s_cbias

    def backward_all(l, grad_rows):
        zero = jnp.zeros((8, CH), F32)
        start = (zero, zero, zero, zero, jnp.zeros((8, HID), F32), zero)
        return lax.fori_loop(0, NI, lambda i, sums: backward(l, grad_rows, i, sums), start)

    def weight_grads(l):
        for m, (a, b) in enumerate(((normed.at[l], gpre), (gbr, act.at[l]))):
            for t in range(3):
                part = tn(a[...], b[:, 256 * t : 256 * t + 256])
                for v in range(2):
                    for r in range(8):
                        piece = m * 48 + (2 * t + v) * 8 + r
                        chunk, slot = divmod(piece, 3)
                        pay[l, chunk // CHUNKS, chunk % CHUNKS, 24 * slot : 24 * slot + 24] = part[
                            24 * r : 24 * r + 24, LANES * v : LANES * v + LANES
                        ]

    def tap_grads(l):
        for part, (cols, base, first) in enumerate(((TC, 0, 0), (TC // 2, TC + 6, TC))):

            @pl.loop(0, SPAN)
            def _(j):
                def body(c, sums):
                    sums = list(sums)
                    for o in range(2):
                        col = 2 * c + o
                        gcs = [gcp[i, first + col] for i in range(NI)]
                        for r in range(NI + SPAN - 1):
                            x = qa[l, r, base + col + j]
                            for i in range(NI):
                                if 0 <= r - i < SPAN:
                                    sums[r - i] = sums[r - i] + gcs[i] * x
                    return tuple(sums)

                zero = jnp.zeros((NS, LANES), F32)
                sums = lax.fori_loop(0, cols // 2, body, (zero,) * SPAN)
                for r in range(SPAN):
                    taps[part, r * SPAN + j] = sums[r]

    def small_grads(l, sums):
        s_gain, s_shift, s_dbias, s_scale, s_ubias, s_cbias = sums
        small[...] = jnp.zeros((LANES, LANES), F32)
        small[:TAPS] = jnp.sum(taps[0], axis=1)
        rest = jnp.sum(taps[1], axis=1)
        small[TAPS : 2 * TAPS, :REST] = rest[:, :REST] + rest[:, REST:]
        for at, v in ((ROW_CBIAS, s_cbias), (ROW_GAIN, s_gain), (ROW_SHIFT, s_shift),
                      (ROW_DBIAS, s_dbias), (ROW_SCALE, s_scale)):
            v = jnp.sum(v, axis=0, keepdims=True)
            small[at : at + 1] = v[:, :LANES]
            small[at + 1 : at + 2, :REST] = v[:, LANES:]
        v = jnp.sum(s_ubias, axis=0, keepdims=True)
        for t in range(6):
            small[ROW_UBIAS + t : ROW_UBIAS + t + 1] = v[:, LANES * t : LANES * t + LANES]
        upper = lax.broadcasted_iota(jnp.int32, (8, LANES), 0) < 4
        for k in range(2 * CHUNKS):
            v = small[8 * (k // 2) : 8 * (k // 2) + 8]
            if k % 2:
                v = pltpu.roll(v, 4, 0)
            pay[l, k // CHUNKS, k % CHUNKS, BIG:] = jnp.where(upper, v, 0.0)

    upper = lax.broadcasted_iota(jnp.int32, (8, LANES), 0) < 4

    def rounded(v, store):
        s = v[BIG:]
        s = s + pltpu.roll(s, 4, 0)
        high = s.astype(BF16).astype(F32)
        store(jnp.concatenate([v[:BIG], jnp.where(upper, high, s - high)], axis=0).astype(BF16))

    def core_copy(l):
        return pltpu.make_async_remote_copy(
            src_ref=pay.at[l, other], dst_ref=corebuf.at[l], send_sem=cs.at[l], recv_sem=cr.at[l],
            device_id=sibling, device_id_type=MESH,
        )

    def plane_copy(l, d):
        index, device = plane_peer(d)
        return pltpu.make_async_remote_copy(
            src_ref=sbuf.at[l, index], dst_ref=rbuf.at[l, d], send_sem=xs.at[l, d], recv_sem=xr.at[l, d],
            device_id=device, device_id_type=MESH,
        )

    def z_copy(l, d):
        return pltpu.make_async_remote_copy(
            src_ref=zbuf.at[l, z], dst_ref=zbuf.at[l, z], send_sem=zs.at[l, d], recv_sem=zr.at[l, z],
            device_id=z_peer(d)[1], device_id_type=MESH,
        )

    def z_arrival(l, d):
        pz, device = z_peer(d)
        return pltpu.make_async_remote_copy(
            src_ref=zbuf.at[l, pz], dst_ref=zbuf.at[l, pz], send_sem=zs.at[l, d], recv_sem=zr.at[l, pz],
            device_id=device, device_id_type=MESH,
        )

    def gather_copy(l, d):
        return pltpu.make_async_remote_copy(
            src_ref=result.at[l, core, me], dst_ref=result.at[l, core, me], send_sem=gs.at[l, d],
            recv_sem=gr.at[l, me], device_id=plane_peer(d)[1], device_id_type=MESH,
        )

    def gather_arrival(l, d):
        index, device = plane_peer(d)
        return pltpu.make_async_remote_copy(
            src_ref=result.at[l, core, index], dst_ref=result.at[l, core, index], send_sem=gs.at[l, d],
            recv_sem=gr.at[l, index], device_id=device, device_id_type=MESH,
        )

    def relay_copy(l, index):
        return pltpu.make_async_remote_copy(
            src_ref=result.at[l, core, index], dst_ref=result.at[l, core, index], send_sem=ls.at[l, index],
            recv_sem=lr.at[l, index], device_id=sibling, device_id_type=MESH,
        )

    def relay_arrival(l, index):
        return pltpu.make_async_remote_copy(
            src_ref=result.at[l, other, index], dst_ref=result.at[l, other, index], send_sem=ls.at[l, index],
            recv_sem=lr.at[l, index], device_id=sibling, device_id_type=MESH,
        )

    def to_plane(l):
        core_copy(l).wait_recv()

        @pl.loop(0, CHUNKS)
        def _(k):
            d = lax.rem(k + 1, CHUNKS)
            index, _ = plane_peer(d)
            v = pay[l, core, index] + corebuf[l, index]

            def store(r):
                sbuf[l, index] = r

            rounded(v, store)

            @pl.when(d > 0)
            def _():
                plane_copy(l, d).start()

    def to_z(l):
        @pl.loop(1, CHUNKS)
        def _(d):
            plane_copy(l, d).wait_recv()

        v = lax.fori_loop(1, CHUNKS, lambda d, v: v + rbuf[l, d].astype(F32), sbuf[l, me].astype(F32))

        def store(r):
            zbuf[l, z] = r

        rounded(v, store)

        @pl.loop(1, NZ)
        def _(d):
            z_copy(l, d).start()

    def to_all(l):
        @pl.loop(1, NZ)
        def _(d):
            z_arrival(l, d).wait_recv()

        v = zbuf[l, 0].astype(F32)
        for k in range(1, NZ):
            v = v + zbuf[l, k].astype(F32)

        def store(r):
            result[l, core, me] = r

        rounded(v * factor, store)

        @pl.loop(1, CHUNKS)
        def _(d):
            gather_copy(l, d).start()

        relay_copy(l, me).start()

    def to_sibling(l):
        @pl.loop(1, CHUNKS)
        def _(d):
            gather_arrival(l, d).wait_recv()
            relay_copy(l, plane_peer(d)[0]).start()

    def finish(l):
        @pl.loop(0, CHUNKS)
        def _(k):
            relay_arrival(l, k).wait_recv()
            relay_copy(l, k).wait_send()

        core_copy(l).wait_send()

        @pl.loop(1, CHUNKS)
        def _(d):
            plane_copy(l, d).wait_send()
            gather_copy(l, d).wait_send()

        @pl.loop(1, NZ)
        def _(d):
            z_copy(l, d).wait_send()

    def flat_rows(plane, i):
        return plane[i, 3 : 3 + TC].reshape(blk, CH)

    def cot_rows(i):
        return grad[rows_of(i)]

    def step_back(l):
        @pl.loop(0, NI)
        def _(i):
            rows = rows_of(i)
            grad[rows] = grad[rows] + conv_rows(i)

    xp[0, :, 3 : 3 + TC] = nn(place[...], feat[...]).reshape(NI, TC, NS, CH)
    halo_start(0, xp.at[0])
    grad[...] = nn(place[...], cot[...])
    halo_wait(0)
    assemble(0, xp.at[0], qa.at[0])
    convolve(qa.at[0], wexp, 0)

    def keep(i, new):
        xp[1, i, 3 : 3 + TC] = new.astype(F32).reshape(TC, NS, CH)

    @pl.loop(0, NI)
    def _(i):
        forward(0, xp.at[0], keep, i)

    halo_start(1, xp.at[1])
    halo_wait(1)
    assemble(1, xp.at[1], qa.at[1])
    convolve(qa.at[1], wexp, 1)

    def keep_out(i, new):
        outq[rows_of(i)] = new

    @pl.loop(0, NI)
    def _(i):
        forward(1, xp.at[1], keep_out, i)

    sums = backward_all(1, cot_rows)
    halo_start(2, gx)
    weight_grads(1)
    tap_grads(1)
    small_grads(1, sums)
    core_copy(1).start()
    out_ref[...] = tn(place[...], outq[...]).astype(BF16)
    halo_wait(2)
    assemble(2, gx, qg)
    convolve(qg, wflip, 1)
    step_back(1)
    to_plane(1)
    sums = backward_all(0, cot_rows)
    halo_start(3, gx)
    to_z(1)
    weight_grads(0)
    to_all(1)
    tap_grads(0)
    small_grads(0, sums)
    core_copy(0).start()
    to_sibling(1)
    halo_wait(3)
    assemble(3, gx, qg)
    to_plane(0)
    convolve(qg, wflip, 0)
    step_back(0)
    to_z(0)
    g = grad[...]
    high = g.astype(BF16)
    g = g - high.astype(F32)
    mid = g.astype(BF16)
    low = (g - mid.astype(F32)).astype(BF16)
    gfeat_ref[...] = tn(place[...], high) + (tn(place[...], mid) + tn(place[...], low))
    to_all(0)
    to_sibling(0)
    for n in range(4):
        halo_done(n)
    finish(1)
    finish(0)


def on_device(features, cotangent, dw_kernel, conv_bias, ln_gain, ln_shift, up_weight, up_bias,
              down_weight, down_bias, layer_scale):
    depth = dw_kernel.shape[0]
    pixel_total = PX * lax.axis_size("slide") * lax.axis_size("ty") * lax.axis_size("tx")
    place, edges, spread = (jnp.asarray(v, BF16) for v in one_hots())
    flat = dw_kernel.reshape(depth, TAPS, CH)
    wexp = jnp.stack([flat[..., :LANES], jnp.concatenate([flat[..., LANES:]] * 2, axis=-1)], axis=1)
    wexp = jnp.broadcast_to(wexp[:, :, :, None, :], (depth, 2, TAPS, NS, LANES))
    wflip = wexp[:, :, ::-1]
    vmem = pl.BlockSpec(memory_space=pltpu.VMEM)
    dma = pltpu.SemaphoreType.DMA
    plane = (NI, TC + 6, NS, CH)
    wide = (NI + 6, WIDE, NS, LANES)
    out, gfeat, result = pl.pallas_call(
        functools.partial(kernel, 1.0 / math.sqrt(pixel_total)),
        out_shape=(
            jax.ShapeDtypeStruct((PX, CH), BF16),
            jax.ShapeDtypeStruct((PX, CH), F32),
            jax.ShapeDtypeStruct((depth, 2, CHUNKS, ROWS, LANES), BF16),
        ),
        in_specs=[vmem] * 15,
        out_specs=(vmem,) * 3,
        scratch_shapes=[
            pltpu.VMEM((2, *plane), F32),
            pltpu.VMEM(plane, F32),
            pltpu.VMEM((2, *wide), F32),
            pltpu.VMEM(wide, F32),
            pltpu.VMEM((NI, PACK, NS, LANES), F32),
            pltpu.VMEM((TC * NS, CH), F32),
            pltpu.VMEM((2, PX, CH), F32),
            pltpu.VMEM((2, PX, 1), F32),
            pltpu.VMEM((2, PX, CH), BF16),
            pltpu.VMEM((2, PX, HID), BF16),
            pltpu.VMEM((2, PX, HID), F32),
            pltpu.VMEM((2, PX, CH), F32),
            pltpu.VMEM((PX, CH), BF16),
            pltpu.VMEM((PX, HID), BF16),
            pltpu.VMEM((NI, PACK, NS, LANES), F32),
            pltpu.VMEM((2, 3, TC + 6, NS, CH), F32),
            pltpu.VMEM((2, TAPS, NS, LANES), F32),
            pltpu.VMEM((LANES, LANES), F32),
            pltpu.VMEM((PX, CH), F32),
            pltpu.VMEM((PX, CH), BF16),
            pltpu.VMEM((2, 2, CHUNKS, ROWS, LANES), F32),
            pltpu.VMEM((2, CHUNKS, ROWS, LANES), F32),
            pltpu.VMEM((2, CHUNKS, ROWS, LANES), BF16),
            pltpu.VMEM((2, CHUNKS, ROWS, LANES), BF16),
            pltpu.VMEM((2, NZ, ROWS, LANES), BF16),
            pltpu.VMEM((4, 2, 3, TR, CH), BF16),
            pltpu.VMEM((4, 2, 3, TC, CH), BF16),
            pltpu.VMEM((4, 2, 3, TR, CH), BF16),
            pltpu.VMEM((4, 6, 3, TC, CH), BF16),
            dma((4, 8)), dma((4, 8)),
            dma((2,)), dma((2,)),
            dma((2, CHUNKS)), dma((2, CHUNKS)),
            dma((2, NZ)), dma((2, NZ)),
            dma((2, CHUNKS)), dma((2, CHUNKS)),
            dma((2, CHUNKS)), dma((2, CHUNKS)),
        ],
        compiler_params=pltpu.CompilerParams(
            collective_id=0, has_side_effects=True, vmem_limit_bytes=56 * 2**20
        ),
    )(
        features.reshape(PX, CH), cotangent.reshape(PX, CH), wexp, wflip, conv_bias, ln_gain, ln_shift,
        up_weight, up_bias, down_weight, down_bias, layer_scale, place, edges, spread,
    )
    result = result.reshape(depth, 2 * CHUNKS, ROWS, LANES)
    big = result[:, :, :BIG].reshape(depth, 2, 6, CH, LANES).astype(F32)
    grad_up = big[:, 0].transpose(0, 2, 1, 3).reshape(depth, CH, HID)
    grad_down = big[:, 1].transpose(0, 1, 3, 2).reshape(depth, HID, CH)
    few = result[:, :, BIG:].astype(F32)
    few = (few[:, :, :4] + few[:, :, 4:]).reshape(depth, LANES, LANES)
    grad_taps = jnp.concatenate([few[:, :TAPS], few[:, TAPS : 2 * TAPS, :REST]], axis=-1)

    def vector(at):
        return jnp.concatenate([few[:, at], few[:, at + 1, :REST]], axis=-1)

    return (
        out.reshape(1, TR, TC, CH),
        gfeat.reshape(1, TR, TC, CH),
        grad_taps.reshape(depth, SPAN, SPAN, CH),
        vector(ROW_CBIAS),
        vector(ROW_GAIN),
        vector(ROW_SHIFT),
        grad_up,
        few[:, ROW_UBIAS : ROW_UBIAS + 6].reshape(depth, HID),
        grad_down,
        vector(ROW_DBIAS),
        vector(ROW_SCALE),
    )


def solution(mesh):
    tiled = P("slide", "ty", "tx", None)
    return jax.shard_map(
        on_device,
        mesh=mesh,
        in_specs=(tiled, tiled) + (P(),) * 9,
        out_specs=(tiled, tiled) + (P(),) * 9,
        check_vma=False,
    )
```

time: 507 us -> 105 us (0.21)
  waiting for transfers between devices: 251 us -> 0 us
  Pallas kernels: 0 us -> 89.2 us
  blocking collectives: 84.3 us -> 0 us
  other arithmetic: 55 us -> 4.23 us
  starting transfers between devices: 44.7 us -> 0 us
  local copies, waits for them, and re-layouts: 32.5 us -> 10.5 us
  matrix products: 19 us -> 0 us
  between operations: 17.1 us -> 0.76 us
    psum x1 -> x0, waiting for transfers between devices: 244 us -> none  [on_device(): stacked = lax.psum(stacked, ('slide', 'ty', 'tx'))]
    pallas_call x0 -> x1, Pallas kernels: none -> 89.2 us  [on_device(): pl.pallas_call(functools.partial(kernel, 1.0 / math.sqrt(pixel_total)), o...]
    psum x1 -> x0, blocking collectives: 84.3 us -> none  [on_device(): stacked = lax.psum(stacked, ('slide', 'ty', 'tx'))]
    ppermute x16 -> x0, starting transfers between devices: 44.6 us -> none  [the longest x8 30.9 us: with_halo(): lax.ppermute(tail, axis, [(i, (i + 1) % count) for i in range(ends)])]
    reduce_sum x14 -> x0, other arithmetic: 31.3 us -> none  [the longest x2 11.4 us: block_forward(): row_mean = jnp.mean(flat_rows, axis=1, keepdims=True)]
    dot_general x12 -> x0, matrix products: 19 us -> none  [the longest x2 4.37 us: block_backward(): lax.dot_general(normed, grad_pre, (((0,), (0,)), ((), ())), preferred_ele...]
    slice x23 -> x7, local copies, waits for them, and re-layouts: 15.4 us -> 3.06 us  [the longest x1 1.37 us: on_device(): big = result[:, :, :BIG].reshape(depth, 2, 6, CH, LANES).astype(F32)]
    mul x9 -> x0, other arithmetic: 8 us -> none  [on_device(): scaled_grads = tuple((member * factor for member in stacked))]
  transfers between devices with their start and end apart: 17 -> 0, of which waited for: 4 -> 0; matrix products, arithmetic and copies ran while one was open for 8% -> 0% of each run, Pallas kernels for 0% -> 0%
where the time goes in v1:
time: 105 us
  Pallas kernels  89.2 us (85%)
  local copies, waits for them, and re-layouts  10.5 us (10%)
  other arithmetic  4.23 us (4%)
    pallas_call x1, Pallas kernels, on_device(): pl.pallas_call(functools.partial(kernel, 1.0 / math.sqrt(pixel_total)), o...  89.2 us
    unnamed x15, local copies, waits for them, and re-layouts  3.54 us
    concatenate x5, other arithmetic, vector(): return jnp.concatenate([few[:, at], few[:, at + 1, :REST]], axis=-1)  2.91 us

profile of v1, /device:TPU:1, one launch (start us, length us, event | category | flops | bytes accessed | tf_op | source)
XLA Modules:
  0.0 104.7 jit_solution(13045220064962080251)
XLA Ops:
  0.6 0.0 copy-start.1
  0.7 0.9 slice.84
  1.5 0.8 slice.85
  2.3 0.1 maximum_bitcast_fusion
  2.4 0.1 broadcast_in_dim.2.wexp
  2.5 0.0 copy-done.1
  2.5 0.0 copy-start
  2.5 1.2 %copy.53.down = bf16[2,768,192]{2,1,0:T(8,128)(2,1)} copy(bf16[2,768,192]{1,2,0:T(8,128)(2,1)S(1)} %copy-done.1) | data formatting | bytes 1179648 | tf_op args[8]
  3.7 0.9 rev.3.wflip
  4.7 0.0 copy-done
  4.7 89.2 %shard_map.221 = (bf16[512,192]{1,0:T(8,128)(2,1)}, f32[512,192]{1,0:T(8,128)}, bf16[2,2,16,80,128]{4,3,2,1,0:T(8,128)(2,1)}) custom-call(bf16[512,192]{1,0:T(8,128)(2,1)} %bitcast.70, bf16[512,192]{1,0:T(8,128)(2,1)} %bitcast.71, f32[2,2,49,8,128]{4,3,2,1,0:T(8,128)} %copy-done, f32[2,2,49,8,128]{4,3,2,1,0:T(8,128)} %rev.3.wflip, f32[2,192]{1,0:T(2,128)} %cbias.1, ...), custom_call_target="tpu_custom_call" | custom-call | tf_op jit(solution)/shard_map/pallas_call | solution.py:580
  93.9 0.9 slice_convert_fusion
  94.8 1.4 %slice.97 = bf16[2,32,72,128]{3,2,1,0:T(8,128)(2,1)S(1)} slice(bf16[2,32,80,128]{3,2,1,0:T(8,128)(2,1)} %bitcast.61), slice={[0:2], [0:32], [0:72], [0:128]} | slice | bytes 2359296 | tf_op jit(solution)/shard_map/slice | solution.py:634
  96.3 0.6 pad_maximum_fusion.6
  96.8 0.6 pad_maximum_fusion.5
  97.4 0.6 pad_maximum_fusion.3
  98.0 0.6 pad_maximum_fusion.4
  98.6 0.6 pad_maximum_fusion.2
  99.2 0.6 copy.82
  99.8 0.7 copy.54
  100.5 0.3 convert.1
  100.8 0.2 slice_bitcast_fusion
  101.0 1.1 %copy.80 = f32[2,6,24,8,128]{4,3,1,2,0:T(8,128)} copy(f32[2,6,24,8,128]{4,3,2,1,0:T(8,128)S(1)} %get-tuple-element.17) | data formatting | bytes 2359296 | tf_op jit(solution)/shard_map/reshape | solution.py:636
  102.1 0.0 copy-start.3
  102.1 0.0 copy-start.2
  102.1 1.1 %copy.81 = f32[2,6,24,8,128]{4,3,1,2,0:T(8,128)} copy(f32[2,6,24,8,128]{4,3,2,1,0:T(8,128)S(1)} %get-tuple-element.18) | data formatting | bytes 2359296 | tf_op jit(solution)/shard_map/reshape | solution.py:635
  103.2 0.0 copy-done.3
  103.2 0.7 copy.85
  103.9 0.0 copy-done.2
  103.9 0.8 copy.86
  (9 shorter events, 0.1 us)
Async XLA Ops:
  0.6 1.9 %copy-start.1 = (bf16[2,768,192]{1,2,0:T(8,128)(2,1)S(1)}, bf16[2,768,192]{1,2,0:T(8,128)(2,1)}, u32[]{:S(2)}) copy-start(bf16[2,768,192]{1,2,0:T(8,128)(2,1)} %param.22) | copy-start | bytes 1769476
  2.5 2.1 %copy-start = (f32[2,2,49,8,128]{4,3,2,1,0:T(8,128)}, f32[2,2,49,8,128]{4,3,2,1,0:T(8,128)S(1)}, u32[]{:S(2)}) copy-start(f32[2,2,49,8,128]{4,3,2,1,0:T(8,128)S(1)} %broadcast_in_dim.2.wexp) | copy-start | bytes 2408452
  102.1 1.1 %copy-start.3 = (bf16[512,192]{1,0:T(8,128)(2,1)S(1)}, bf16[512,192]{1,0:T(8,128)(2,1)}, u32[]{:S(2)}) copy-start(bf16[512,192]{1,0:T(8,128)(2,1)} %get-tuple-element.14) | copy-start | bytes 589828
  102.1 1.8 %copy-start.2 = (f32[512,192]{1,0:T(8,128)S(1)}, f32[512,192]{1,0:T(8,128)}, u32[]{:S(2)}) copy-start(f32[512,192]{1,0:T(8,128)} %get-tuple-element.15) | copy-start | bytes 1179652

commit v2 on v1

--- a/solution.py
+++ b/solution.py
@@ -72,10 +72,10 @@
 
 def kernel(
     factor,
-    feat, cot, wexp, wflip, cbias, gain, shift, up, ubias, down, dbias, scale, place, edges, spread,
+    feat, cot, dw, cbias, gain, shift, up, ubias, down, dbias, scale, place, edges, spread,
     out_ref, gfeat_ref, result,
     xp, gx, qa, qg, cbuf, conv, unit, inv, normed, act, slope, branch, gbr, gpre, gcp, tq, taps, small,
-    grad, outq, pay, corebuf, sbuf, rbuf, zbuf,
+    grad, outq, wexp, pay, corebuf, sbuf, rbuf, zbuf,
     csend, rsend, crecv, rrecv,
     hs, hr, cs, cr, xs, xr, zs, zr, gs, gr, ls, lr,
 ):
@@ -198,7 +198,7 @@
         def _(k):
             fill(TC + 6 + k, pair(plane, slice(None), k), pair(tq, 0, slice(None), k), pair(tq, 1, slice(None), k))
 
-    def convolve(q, weights, l):
+    def convolve(q, l, flip):
         def columns(part, t, base):
             sums = [[None, None] for _ in range(NI)]
             for j2 in range(SPAN + 1):
@@ -210,7 +210,8 @@
                         for o in range(2):
                             if not 0 <= j2 - o < SPAN:
                                 continue
-                            term = x * weights[l, part, (r - i) * SPAN + j2 - o]
+                            tap = (r - i) * SPAN + j2 - o
+                            term = x * wexp[l, part, TAPS - 1 - tap if flip else tap]
                             sums[i][o] = term if sums[i][o] is None else sums[i][o] + term
             for i in range(NI):
                 for o in range(2):
@@ -252,7 +253,7 @@
         slope[l, rows] = cdf + pre * INV_ROOT_TAU * jnp.exp(-0.5 * pre * pre)
         ab = (pre * cdf).astype(BF16)
         act[l, rows] = ab
-        br = nn(ab, down[l]) + dbias[l : l + 1]
+        br = nt(ab, down[l]) + dbias[l : l + 1]
         branch[l, rows] = br
         before = plane[i, 3 : 3 + TC].reshape(blk, CH)
         new = (before + scale[l : l + 1] * br).astype(BF16)
@@ -270,7 +271,7 @@
         gb = (g * scale[l : l + 1]).astype(BF16)
         gbr[rows] = gb
         s_dbias = s_dbias + fold(gb.astype(F32))
-        gp = (nt(gb, down[l]) * slope[l, rows]).astype(BF16)
+        gp = (nn(gb, down[l]) * slope[l, rows]).astype(BF16)
         gpre[rows] = gp
         s_ubias = s_ubias + fold(gp.astype(F32))
         gn = nt(gp, up[l])
@@ -500,9 +501,18 @@
     xp[0, :, 3 : 3 + TC] = nn(place[...], feat[...]).reshape(NI, TC, NS, CH)
     halo_start(0, xp.at[0])
     grad[...] = nn(place[...], cot[...])
+
+    @pl.loop(0, TAPS)
+    def _(t):
+        for l in range(2):
+            tap = dw[t, l : l + 1]
+            rest = tap[:, LANES:]
+            wexp[l, 0, t] = jnp.broadcast_to(tap[:, :LANES], (NS, LANES))
+            wexp[l, 1, t] = jnp.broadcast_to(jnp.concatenate([rest, rest], axis=1), (NS, LANES))
+
     halo_wait(0)
     assemble(0, xp.at[0], qa.at[0])
-    convolve(qa.at[0], wexp, 0)
+    convolve(qa.at[0], 0, False)
 
     def keep(i, new):
         xp[1, i, 3 : 3 + TC] = new.astype(F32).reshape(TC, NS, CH)
@@ -514,7 +524,7 @@
     halo_start(1, xp.at[1])
     halo_wait(1)
     assemble(1, xp.at[1], qa.at[1])
-    convolve(qa.at[1], wexp, 1)
+    convolve(qa.at[1], 1, False)
 
     def keep_out(i, new):
         outq[rows_of(i)] = new
@@ -532,7 +542,7 @@
     out_ref[...] = tn(place[...], outq[...]).astype(BF16)
     halo_wait(2)
     assemble(2, gx, qg)
-    convolve(qg, wflip, 1)
+    convolve(qg, 1, True)
     step_back(1)
     to_plane(1)
     sums = backward_all(0, cot_rows)
@@ -547,7 +557,7 @@
     halo_wait(3)
     assemble(3, gx, qg)
     to_plane(0)
-    convolve(qg, wflip, 0)
+    convolve(qg, 0, True)
     step_back(0)
     to_z(0)
     g = grad[...]
@@ -564,15 +574,40 @@
     finish(0)
 
 
+def unpack(out_in, gfeat_in, result, out, gfeat, gtaps, gcbias, ggain, gshift, gup, gubias, gdown, gdbias, gscale, few):
+    out[...] = out_in[...]
+    gfeat[...] = gfeat_in[...]
+    upper = lax.broadcasted_iota(jnp.int32, (8, LANES), 0) < 4
+    for l in range(2):
+        for piece in range(96):
+            chunk, slot = divmod(piece, 3)
+            m, piece = divmod(piece, 48)
+            t, r = divmod(piece, 8)
+            value = result[l, chunk // CHUNKS, chunk % CHUNKS, 24 * slot : 24 * slot + 24].astype(F32)
+            (gup, gdown)[m][l, 24 * r : 24 * r + 24, LANES * t : LANES * t + LANES] = value
+        for k in range(CHUNKS):
+            pair = []
+            for chunk in (2 * k, 2 * k + 1):
+                v = result[l, chunk // CHUNKS, chunk % CHUNKS, BIG:].astype(F32)
+                pair.append(v + pltpu.roll(v, 4, 0))
+            few[8 * k : 8 * k + 8] = jnp.where(upper, pair[0], pair[1])
+        for t in range(TAPS):
+            gtaps[t, l : l + 1, :LANES] = few[t : t + 1]
+            gtaps[t, l : l + 1, LANES:] = few[TAPS + t : TAPS + t + 1, :REST]
+        for at, ref in ((ROW_CBIAS, gcbias), (ROW_GAIN, ggain), (ROW_SHIFT, gshift),
+                        (ROW_DBIAS, gdbias), (ROW_SCALE, gscale)):
+            ref[l : l + 1, :LANES] = few[at : at + 1]
+            ref[l : l + 1, LANES:] = few[at + 1 : at + 2, :REST]
+        for t in range(6):
+            gubias[l : l + 1, LANES * t : LANES * t + LANES] = few[ROW_UBIAS + t : ROW_UBIAS + t + 1]
+
+
 def on_device(features, cotangent, dw_kernel, conv_bias, ln_gain, ln_shift, up_weight, up_bias,
               down_weight, down_bias, layer_scale):
     depth = dw_kernel.shape[0]
     pixel_total = PX * lax.axis_size("slide") * lax.axis_size("ty") * lax.axis_size("tx")
     place, edges, spread = (jnp.asarray(v, BF16) for v in one_hots())
-    flat = dw_kernel.reshape(depth, TAPS, CH)
-    wexp = jnp.stack([flat[..., :LANES], jnp.concatenate([flat[..., LANES:]] * 2, axis=-1)], axis=1)
-    wexp = jnp.broadcast_to(wexp[:, :, :, None, :], (depth, 2, TAPS, NS, LANES))
-    wflip = wexp[:, :, ::-1]
+    taps = dw_kernel.reshape(depth, TAPS, CH).transpose(1, 0, 2)
     vmem = pl.BlockSpec(memory_space=pltpu.VMEM)
     dma = pltpu.SemaphoreType.DMA
     plane = (NI, TC + 6, NS, CH)
@@ -584,7 +619,7 @@
             jax.ShapeDtypeStruct((PX, CH), F32),
             jax.ShapeDtypeStruct((depth, 2, CHUNKS, ROWS, LANES), BF16),
         ),
-        in_specs=[vmem] * 15,
+        in_specs=[vmem] * 14,
         out_specs=(vmem,) * 3,
         scratch_shapes=[
             pltpu.VMEM((2, *plane), F32),
@@ -607,6 +642,7 @@
             pltpu.VMEM((LANES, LANES), F32),
             pltpu.VMEM((PX, CH), F32),
             pltpu.VMEM((PX, CH), BF16),
+            pltpu.VMEM((2, 2, TAPS, NS, LANES), F32),
             pltpu.VMEM((2, 2, CHUNKS, ROWS, LANES), F32),
             pltpu.VMEM((2, CHUNKS, ROWS, LANES), F32),
             pltpu.VMEM((2, CHUNKS, ROWS, LANES), BF16),
@@ -627,32 +663,36 @@
             collective_id=0, has_side_effects=True, vmem_limit_bytes=56 * 2**20
         ),
     )(
-        features.reshape(PX, CH), cotangent.reshape(PX, CH), wexp, wflip, conv_bias, ln_gain, ln_shift,
-        up_weight, up_bias, down_weight, down_bias, layer_scale, place, edges, spread,
+        features.reshape(PX, CH), cotangent.reshape(PX, CH), taps, conv_bias, ln_gain, ln_shift,
+        up_weight, up_bias, down_weight.transpose(0, 2, 1), down_bias, layer_scale, place, edges, spread,
     )
-    result = result.reshape(depth, 2 * CHUNKS, ROWS, LANES)
-    big = result[:, :, :BIG].reshape(depth, 2, 6, CH, LANES).astype(F32)
-    grad_up = big[:, 0].transpose(0, 2, 1, 3).reshape(depth, CH, HID)
-    grad_down = big[:, 1].transpose(0, 1, 3, 2).reshape(depth, HID, CH)
-    few = result[:, :, BIG:].astype(F32)
-    few = (few[:, :, :4] + few[:, :, 4:]).reshape(depth, LANES, LANES)
-    grad_taps = jnp.concatenate([few[:, :TAPS], few[:, TAPS : 2 * TAPS, :REST]], axis=-1)
-
-    def vector(at):
-        return jnp.concatenate([few[:, at], few[:, at + 1, :REST]], axis=-1)
-
+    vector = jax.ShapeDtypeStruct((depth, CH), F32)
+    weight = jax.ShapeDtypeStruct((depth, CH, HID), F32)
+    out, gfeat, gtaps, gcbias, ggain, gshift, gup, gubias, gdown, gdbias, gscale = pl.pallas_call(
+        unpack,
+        out_shape=(
+            jax.ShapeDtypeStruct((PX, CH), BF16),
+            jax.ShapeDtypeStruct((PX, CH), F32),
+            jax.ShapeDtypeStruct((TAPS, depth, CH), F32),
+            vector, vector, vector, weight, jax.ShapeDtypeStruct((depth, HID), F32), weight, vector, vector,
+        ),
+        in_specs=[vmem] * 3,
+        out_specs=(vmem,) * 11,
+        scratch_shapes=[pltpu.VMEM((LANES, LANES), F32)],
+        compiler_params=pltpu.CompilerParams(vmem_limit_bytes=24 * 2**20),
+    )(out, gfeat, result)
     return (
         out.reshape(1, TR, TC, CH),
         gfeat.reshape(1, TR, TC, CH),
-        grad_taps.reshape(depth, SPAN, SPAN, CH),
-        vector(ROW_CBIAS),
-        vector(ROW_GAIN),
-        vector(ROW_SHIFT),
-        grad_up,
-        few[:, ROW_UBIAS : ROW_UBIAS + 6].reshape(depth, HID),
-        grad_down,
-        vector(ROW_DBIAS),
-        vector(ROW_SCALE),
+        gtaps.transpose(1, 0, 2).reshape(depth, SPAN, SPAN, CH),
+        gcbias,
+        ggain,
+        gshift,
+        gup,
+        gubias,
+        gdown.transpose(0, 2, 1),
+        gdbias,
+        gscale,
     )
 
 

time: 105 us -> 94.4 us (0.90)
  local copies, waits for them, and re-layouts: 10.5 us -> 3.3 us
  other arithmetic: 4.23 us -> 0 us
    slice x7 -> x0, local copies, waits for them, and re-layouts: 3.06 us -> none  [the longest x1 1.37 us: on_device(): big = result[:, :, :BIG].reshape(depth, 2, 6, CH, LANES).astype(F32)]
    concatenate x6 -> x0, other arithmetic: 2.92 us -> none  [the longest x5 2.91 us: vector(): return jnp.concatenate([few[:, at], few[:, at + 1, :REST]], axis=-1)]
    reshape x2 -> x0, local copies, waits for them, and re-layouts: 2.2 us -> none  [the longest x1 1.1 us: on_device(): grad_down = big[:, 1].transpose(0, 1, 3, 2).reshape(depth, HID, CH)]
    pallas_call x0 -> x1, Pallas kernels: none -> 1.74 us  [on_device(): pl.pallas_call(unpack, out_shape=(jax.ShapeDtypeStruct((PX, CH), BF16), j...]
    convert_element_type x2 -> x0, other arithmetic: 1.18 us -> none  [the longest x1 0.92 us: on_device(): few = result[:, :, BIG:].astype(F32)]
    unnamed x15 -> x6, local copies, waits for them, and re-layouts: 3.54 us -> 3.3 us
where the time goes in v2:
time: 94.4 us; the launch traced here: 94.2 us
  Pallas kernels  90.2 us (96%)
  local copies, waits for them, and re-layouts  3.3 us (3%)
    pallas_call x1, Pallas kernels, on_device(): pl.pallas_call(functools.partial(kernel, 1.0 / math.sqrt(pixel_total)), o...  88.5 us
    unnamed x6, local copies, waits for them, and re-layouts  3.3 us

profile of v2, /device:TPU:1, one launch (start us, length us, event | category | flops | bytes accessed | tf_op | source)
XLA Modules:
  0.0 94.2 jit_solution(119736438629458708)
XLA Ops:
  0.6 88.5 %shard_map.221 = (bf16[512,192]{1,0:T(8,128)(2,1)}, f32[512,192]{1,0:T(8,128)}, bf16[2,2,16,80,128]{4,3,2,1,0:T(8,128)(2,1)}) custom-call(bf16[512,192]{1,0:T(8,128)(2,1)} %bitcast.13, bf16[512,192]{1,0:T(8,128)(2,1)} %bitcast.14, f32[49,2,192]{2,1,0:T(2,128)} %bitcast.15, f32[2,192]{1,0:T(2,128)} %cbias.1, f32[2,192]{1,0:T(2,128)} %gain.1, f32[2,192]{1,0:T(2,128)} %shift.1, ...), custom_call_target="tpu_custom_call" | custom-call | tf_op jit(solution)/shard_map/pallas_call | solution.py:615
  89.1 0.0 copy-start
  89.2 1.3 %copy-done = bf16[2,2,16,80,128]{4,3,2,1,0:T(8,128)(2,1)S(1)} copy-done((bf16[2,2,16,80,128]{4,3,2,1,0:T(8,128)(2,1)S(1)}, bf16[2,2,16,80,128]{4,3,2,1,0:T(8,128)(2,1)}, u32[]{:S(2)}) %copy-start) | copy-done | bytes 1310744
  90.5 0.0 copy-start.1
  90.5 1.0 %copy-done.1 = f32[512,192]{1,0:T(8,128)S(1)} copy-done((f32[512,192]{1,0:T(8,128)S(1)}, f32[512,192]{1,0:T(8,128)}, u32[]{:S(2)}) %copy-start.1) | copy-done | bytes 393240
  91.5 0.0 copy-start.2
  91.5 0.9 %copy-done.2 = bf16[512,192]{1,0:T(8,128)(2,1)S(1)} copy-done((bf16[512,192]{1,0:T(8,128)(2,1)S(1)}, bf16[512,192]{1,0:T(8,128)(2,1)}, u32[]{:S(2)}) %copy-start.2) | copy-done | bytes 196632
  92.5 1.7 %shard_map.222 = (bf16[512,192]{1,0:T(8,128)(2,1)}, f32[512,192]{1,0:T(8,128)}, f32[49,2,192]{2,1,0:T(2,128)}, f32[2,192]{1,0:T(2,128)}, f32[2,192]{1,0:T(2,128)...) custom-call(bf16[512,192]{1,0:T(8,128)(2,1)S(1)} %copy-done.2, ...), custom_call_target="tpu_custom_call" | custom-call | tf_op jit(solution)/shard_map/pallas_call | solution.py:671
Async XLA Ops:
  89.1 1.3 %copy-start = (bf16[2,2,16,80,128]{4,3,2,1,0:T(8,128)(2,1)S(1)}, bf16[2,2,16,80,128]{4,3,2,1,0:T(8,128)(2,1)}, u32[]{:S(2)}) copy-start(bf16[2,2,16,80,128]{4,3,2,1,0:T(8,128)(2,1)} %get-tuple-element.27.result) | copy-start | bytes 3932164
  90.5 1.0 %copy-start.1 = (f32[512,192]{1,0:T(8,128)S(1)}, f32[512,192]{1,0:T(8,128)}, u32[]{:S(2)}) copy-start(f32[512,192]{1,0:T(8,128)} %get-tuple-element.26.gfeat_in) | copy-start | bytes 1179652
  91.5 0.9 %copy-start.2 = (bf16[512,192]{1,0:T(8,128)(2,1)S(1)}, bf16[512,192]{1,0:T(8,128)(2,1)}, u32[]{:S(2)}) copy-start(bf16[512,192]{1,0:T(8,128)(2,1)} %get-tuple-element.25.out_in) | copy-start | bytes 589828

commit v3 on v2

--- a/solution.py
+++ b/solution.py
@@ -26,8 +26,9 @@
 REST = CH - LANES
 PACK = TC + TC // 2
 WIDE = (TC + 2 * MARGIN) + (TC // 2 + 2 * MARGIN)
-BIG = 72
-ROWS = 80
+PARTS = (32, 48)
+DTILES = 128
+SMALL_AT = 40
 CHUNKS = 16
 NZ = 8
 HALOS = ((-1, -1), (-1, 0), (-1, 1), (1, -1), (1, 0), (1, 1), (0, -1), (0, 1))
@@ -72,10 +73,12 @@
 
 def kernel(
     factor,
-    feat, cot, dw, cbias, gain, shift, up, ubias, down, dbias, scale, place, edges, spread,
-    out_ref, gfeat_ref, result,
+    feat_in, cot_in, dw_in, cbias, gain, shift, up_in, ubias, down_in, dbias, scale, place_in, edges_in, spread_in,
+    out_to, gfeat_to, result0_to, result1_to,
+    feat, cot, dw, up, down, place, edges, spread, out_ref, gfeat_ref, result0, result1, ins, outs,
     xp, gx, qa, qg, cbuf, conv, unit, inv, normed, act, slope, branch, gbr, gpre, gcp, tq, taps, small,
-    grad, outq, wexp, pay, corebuf, sbuf, rbuf, zbuf,
+    grad, outq, wexp,
+    pay0, pay1, core0, core1, sbuf0, sbuf1, rbuf0, rbuf1, zbuf0, zbuf1,
     csend, rsend, crecv, rrecv,
     hs, hr, cs, cr, xs, xr, zs, zr, gs, gr, ls, lr,
 ):
@@ -115,6 +118,20 @@
     @pl.loop(1, NZ)
     def _(d):
         greet(z_peer(d)[1])
+
+    arrivals = {}
+    loads = ((feat_in, feat), (place_in, place), (edges_in, edges), (cot_in, cot), (dw_in, dw), (spread_in, spread),
+             (up_in, up), (down_in, down))
+    for k, (src, dst) in enumerate(loads):
+        arrivals[id(dst)] = pltpu.make_async_copy(src, dst, ins.at[k])
+        arrivals[id(dst)].start()
+
+    def ready(*refs):
+        for ref in refs:
+            arrivals[id(ref)].wait()
+
+    def leave(k, src, dst):
+        return pltpu.make_async_copy(src, dst, outs.at[k])
 
     def there(dy, dx):
         flags = []
@@ -259,53 +276,66 @@
         new = (before + scale[l : l + 1] * br).astype(BF16)
         into(i, new)
 
-    def backward(l, grad_rows, i, sums):
-        rows = rows_of(i)
-        g = grad_rows(i)
-        s_gain, s_shift, s_dbias, s_scale, s_ubias, s_cbias = sums
-
-        def fold(v):
-            return jnp.sum(v.reshape(blk // 8, 8, v.shape[1]), axis=0)
-
-        s_scale = s_scale + fold(g * branch[l, rows])
-        gb = (g * scale[l : l + 1]).astype(BF16)
-        gbr[rows] = gb
-        s_dbias = s_dbias + fold(gb.astype(F32))
-        gp = (nn(gb, down[l]) * slope[l, rows]).astype(BF16)
-        gpre[rows] = gp
-        s_ubias = s_ubias + fold(gp.astype(F32))
-        gn = nt(gp, up[l])
-        u = unit[l, rows]
-        gnu = gn * u
-        s_gain = s_gain + fold(gnu)
-        s_shift = s_shift + fold(gn)
-        q = gn * gain[l : l + 1]
-        centred = q - jnp.mean(q, axis=1, keepdims=True) - u * jnp.mean(q * u, axis=1, keepdims=True)
-        gc = (inv[l, rows] * centred).astype(BF16).astype(F32)
-        s_cbias = s_cbias + fold(gc)
-        gx[i, 3 : 3 + TC] = gc.reshape(TC, NS, CH)
-        gcp[i, :TC] = gc[:, :LANES].reshape(TC, NS, LANES)
-        half = blk // 2
-        gcp[i, TC:, :, :REST] = gc[:half, LANES:].reshape(TC // 2, NS, REST)
-        gcp[i, TC:, :, REST:] = gc[half:, LANES:].reshape(TC // 2, NS, REST)
-        return s_gain, s_shift, s_dbias, s_scale, s_ubias, s_cbias
-
-    def backward_all(l, grad_rows):
+    def fold(v):
+        return jnp.sum(v.reshape(blk // 8, 8, v.shape[1]), axis=0)
+
+    def branch_grads(l):
+        def body(i, sums):
+            rows = rows_of(i)
+            g = grad[rows]
+            gb = (g * scale[l : l + 1]).astype(BF16)
+            gbr[rows] = gb
+            return sums[0] + fold(gb.astype(F32)), sums[1] + fold(g * branch[l, rows])
+
+        return lax.fori_loop(0, NI, body, (jnp.zeros((8, CH), F32),) * 2)
+
+    def backward(l):
+        def body(i, sums):
+            rows = rows_of(i)
+            s_gain, s_shift, s_ubias, s_cbias = sums
+            gp = (nn(gbr[rows], down[l]) * slope[l, rows]).astype(BF16)
+            gpre[rows] = gp
+            s_ubias = s_ubias + fold(gp.astype(F32))
+            gn = nt(gp, up[l])
+            u = unit[l, rows]
+            s_gain = s_gain + fold(gn * u)
+            s_shift = s_shift + fold(gn)
+            q = gn * gain[l : l + 1]
+            centred = q - jnp.mean(q, axis=1, keepdims=True) - u * jnp.mean(q * u, axis=1, keepdims=True)
+            gc = (inv[l, rows] * centred).astype(BF16).astype(F32)
+            s_cbias = s_cbias + fold(gc)
+            gx[i, 3 : 3 + TC] = gc.reshape(TC, NS, CH)
+            gcp[i, :TC] = gc[:, :LANES].reshape(TC, NS, LANES)
+            half = blk // 2
+            gcp[i, TC:, :, :REST] = gc[:half, LANES:].reshape(TC // 2, NS, REST)
+            gcp[i, TC:, :, REST:] = gc[half:, LANES:].reshape(TC // 2, NS, REST)
+            return s_gain, s_shift, s_ubias, s_cbias
+
         zero = jnp.zeros((8, CH), F32)
-        start = (zero, zero, zero, zero, jnp.zeros((8, HID), F32), zero)
-        return lax.fori_loop(0, NI, lambda i, sums: backward(l, grad_rows, i, sums), start)
-
-    def weight_grads(l):
-        for m, (a, b) in enumerate(((normed.at[l], gpre), (gbr, act.at[l]))):
-            for t in range(3):
-                part = tn(a[...], b[:, 256 * t : 256 * t + 256])
-                for v in range(2):
-                    for r in range(8):
-                        piece = m * 48 + (2 * t + v) * 8 + r
-                        chunk, slot = divmod(piece, 3)
-                        pay[l, chunk // CHUNKS, chunk % CHUNKS, 24 * slot : 24 * slot + 24] = part[
-                            24 * r : 24 * r + 24, LANES * v : LANES * v + LANES
-                        ]
+        return lax.fori_loop(0, NI, body, (zero, zero, jnp.zeros((8, HID), F32), zero))
+
+    def put(l, index, tile, tiles, pay):
+        chunk, slot = divmod(index, tiles)
+        pay[l, chunk // CHUNKS, chunk % CHUNKS, 8 * slot : 8 * slot + 8] = tile
+
+    def weight_tiles(a, b, store):
+        for t in range(3):
+            part = tn(a[...], b[:, 256 * t : 256 * t + 256])
+            for v in range(2):
+                for r in range(CH // 8):
+                    store((2 * t + v) * (CH // 8) + r, part[8 * r : 8 * r + 8, LANES * v : LANES * v + LANES])
+
+    def down_grads(l):
+        def store(index, tile):
+            if index < DTILES:
+                put(l, index, tile, 4, pay0)
+            else:
+                put(l, index + CH // 8 * 6 - DTILES, tile, 5, pay1)
+
+        weight_tiles(gbr, act.at[l], store)
+
+    def up_grads(l):
+        weight_tiles(normed.at[l], gpre, lambda index, tile: put(l, index, tile, 5, pay1))
 
     def tap_grads(l):
         for part, (cols, base, first) in enumerate(((TC, 0, 0), (TC // 2, TC + 6, TC))):
@@ -329,8 +359,9 @@
                 for r in range(SPAN):
                     taps[part, r * SPAN + j] = sums[r]
 
-    def small_grads(l, sums):
-        s_gain, s_shift, s_dbias, s_scale, s_ubias, s_cbias = sums
+    def small_grads(l, early, sums):
+        s_dbias, s_scale = early
+        s_gain, s_shift, s_ubias, s_cbias = sums
         small[...] = jnp.zeros((LANES, LANES), F32)
         small[:TAPS] = jnp.sum(taps[0], axis=1)
         rest = jnp.sum(taps[1], axis=1)
@@ -348,149 +379,140 @@
             v = small[8 * (k // 2) : 8 * (k // 2) + 8]
             if k % 2:
                 v = pltpu.roll(v, 4, 0)
-            pay[l, k // CHUNKS, k % CHUNKS, BIG:] = jnp.where(upper, v, 0.0)
+            pay1[l, k // CHUNKS, k % CHUNKS, SMALL_AT:] = jnp.where(upper, v, 0.0)
 
     upper = lax.broadcasted_iota(jnp.int32, (8, LANES), 0) < 4
 
-    def rounded(v, store):
-        s = v[BIG:]
+    def rounded(v, part):
+        if part == 0:
+            return v.astype(BF16)
+        s = v[SMALL_AT:]
         s = s + pltpu.roll(s, 4, 0)
         high = s.astype(BF16).astype(F32)
-        store(jnp.concatenate([v[:BIG], jnp.where(upper, high, s - high)], axis=0).astype(BF16))
-
-    def core_copy(l):
+        return jnp.concatenate([v[:SMALL_AT], jnp.where(upper, high, s - high)], axis=0).astype(BF16)
+
+    pays, cores, sbufs, rbufs, zbufs = (pay0, pay1), (core0, core1), (sbuf0, sbuf1), (rbuf0, rbuf1), (zbuf0, zbuf1)
+    results = (result0, result1)
+
+    def core_copy(l, p):
         return pltpu.make_async_remote_copy(
-            src_ref=pay.at[l, other], dst_ref=corebuf.at[l], send_sem=cs.at[l], recv_sem=cr.at[l],
+            src_ref=pays[p].at[l, other], dst_ref=cores[p].at[l], send_sem=cs.at[2 * l + p], recv_sem=cr.at[2 * l + p],
             device_id=sibling, device_id_type=MESH,
         )
 
-    def plane_copy(l, d):
+    def plane_copy(l, p, d):
         index, device = plane_peer(d)
         return pltpu.make_async_remote_copy(
-            src_ref=sbuf.at[l, index], dst_ref=rbuf.at[l, d], send_sem=xs.at[l, d], recv_sem=xr.at[l, d],
+            src_ref=sbufs[p].at[l, index], dst_ref=rbufs[p].at[l, d], send_sem=xs.at[2 * l + p, d], recv_sem=xr.at[2 * l + p, d],
             device_id=device, device_id_type=MESH,
         )
 
-    def z_copy(l, d):
+    def z_copy(l, p, d):
         return pltpu.make_async_remote_copy(
-            src_ref=zbuf.at[l, z], dst_ref=zbuf.at[l, z], send_sem=zs.at[l, d], recv_sem=zr.at[l, z],
+            src_ref=zbufs[p].at[l, z], dst_ref=zbufs[p].at[l, z], send_sem=zs.at[2 * l + p, d], recv_sem=zr.at[2 * l + p, z],
             device_id=z_peer(d)[1], device_id_type=MESH,
         )
 
-    def z_arrival(l, d):
+    def z_arrival(l, p, d):
         pz, device = z_peer(d)
         return pltpu.make_async_remote_copy(
-            src_ref=zbuf.at[l, pz], dst_ref=zbuf.at[l, pz], send_sem=zs.at[l, d], recv_sem=zr.at[l, pz],
+            src_ref=zbufs[p].at[l, pz], dst_ref=zbufs[p].at[l, pz], send_sem=zs.at[2 * l + p, d], recv_sem=zr.at[2 * l + p, pz],
             device_id=device, device_id_type=MESH,
         )
 
-    def gather_copy(l, d):
+    def gather_copy(l, p, d):
         return pltpu.make_async_remote_copy(
-            src_ref=result.at[l, core, me], dst_ref=result.at[l, core, me], send_sem=gs.at[l, d],
-            recv_sem=gr.at[l, me], device_id=plane_peer(d)[1], device_id_type=MESH,
-        )
-
-    def gather_arrival(l, d):
+            src_ref=results[p].at[l, core, me], dst_ref=results[p].at[l, core, me], send_sem=gs.at[2 * l + p, d],
+            recv_sem=gr.at[2 * l + p, me], device_id=plane_peer(d)[1], device_id_type=MESH,
+        )
+
+    def gather_arrival(l, p, d):
         index, device = plane_peer(d)
         return pltpu.make_async_remote_copy(
-            src_ref=result.at[l, core, index], dst_ref=result.at[l, core, index], send_sem=gs.at[l, d],
-            recv_sem=gr.at[l, index], device_id=device, device_id_type=MESH,
-        )
-
-    def relay_copy(l, index):
+            src_ref=results[p].at[l, core, index], dst_ref=results[p].at[l, core, index], send_sem=gs.at[2 * l + p, d],
+            recv_sem=gr.at[2 * l + p, index], device_id=device, device_id_type=MESH,
+        )
+
+    def relay_copy(l, p, index):
         return pltpu.make_async_remote_copy(
-            src_ref=result.at[l, core, index], dst_ref=result.at[l, core, index], send_sem=ls.at[l, index],
-            recv_sem=lr.at[l, index], device_id=sibling, device_id_type=MESH,
-        )
-
-    def relay_arrival(l, index):
+            src_ref=results[p].at[l, core, index], dst_ref=results[p].at[l, core, index], send_sem=ls.at[2 * l + p, index],
+            recv_sem=lr.at[2 * l + p, index], device_id=sibling, device_id_type=MESH,
+        )
+
+    def relay_arrival(l, p, index):
         return pltpu.make_async_remote_copy(
-            src_ref=result.at[l, other, index], dst_ref=result.at[l, other, index], send_sem=ls.at[l, index],
-            recv_sem=lr.at[l, index], device_id=sibling, device_id_type=MESH,
-        )
-
-    def to_plane(l):
-        core_copy(l).wait_recv()
+            src_ref=results[p].at[l, other, index], dst_ref=results[p].at[l, other, index], send_sem=ls.at[2 * l + p, index],
+            recv_sem=lr.at[2 * l + p, index], device_id=sibling, device_id_type=MESH,
+        )
+
+    def to_plane(l, p):
+        core_copy(l, p).wait_recv()
 
         @pl.loop(0, CHUNKS)
         def _(k):
             d = lax.rem(k + 1, CHUNKS)
             index, _ = plane_peer(d)
-            v = pay[l, core, index] + corebuf[l, index]
-
-            def store(r):
-                sbuf[l, index] = r
-
-            rounded(v, store)
+            v = pays[p][l, core, index] + cores[p][l, index]
+            sbufs[p][l, index] = rounded(v, p)
 
             @pl.when(d > 0)
             def _():
-                plane_copy(l, d).start()
-
-    def to_z(l):
+                plane_copy(l, p, d).start()
+
+    def to_z(l, p):
         @pl.loop(1, CHUNKS)
         def _(d):
-            plane_copy(l, d).wait_recv()
-
-        v = lax.fori_loop(1, CHUNKS, lambda d, v: v + rbuf[l, d].astype(F32), sbuf[l, me].astype(F32))
-
-        def store(r):
-            zbuf[l, z] = r
-
-        rounded(v, store)
+            plane_copy(l, p, d).wait_recv()
+
+        v = lax.fori_loop(1, CHUNKS, lambda d, v: v + rbufs[p][l, d].astype(F32), sbufs[p][l, me].astype(F32))
+        zbufs[p][l, z] = rounded(v, p)
 
         @pl.loop(1, NZ)
         def _(d):
-            z_copy(l, d).start()
-
-    def to_all(l):
+            z_copy(l, p, d).start()
+
+    def to_all(l, p):
         @pl.loop(1, NZ)
         def _(d):
-            z_arrival(l, d).wait_recv()
-
-        v = zbuf[l, 0].astype(F32)
+            z_arrival(l, p, d).wait_recv()
+
+        v = zbufs[p][l, 0].astype(F32)
         for k in range(1, NZ):
-            v = v + zbuf[l, k].astype(F32)
-
-        def store(r):
-            result[l, core, me] = r
-
-        rounded(v * factor, store)
+            v = v + zbufs[p][l, k].astype(F32)
+        results[p][l, core, me] = rounded(v * factor, p)
 
         @pl.loop(1, CHUNKS)
         def _(d):
-            gather_copy(l, d).start()
-
-        relay_copy(l, me).start()
-
-    def to_sibling(l):
+            gather_copy(l, p, d).start()
+
+        relay_copy(l, p, me).start()
+
+    def to_sibling(l, p):
         @pl.loop(1, CHUNKS)
         def _(d):
-            gather_arrival(l, d).wait_recv()
-            relay_copy(l, plane_peer(d)[0]).start()
-
-    def finish(l):
+            gather_arrival(l, p, d).wait_recv()
+            relay_copy(l, p, plane_peer(d)[0]).start()
+
+    def finish(l, p):
         @pl.loop(0, CHUNKS)
         def _(k):
-            relay_arrival(l, k).wait_recv()
-            relay_copy(l, k).wait_send()
-
-        core_copy(l).wait_send()
+            relay_arrival(l, p, k).wait_recv()
+            relay_copy(l, p, k).wait_send()
+
+        core_copy(l, p).wait_send()
 
         @pl.loop(1, CHUNKS)
         def _(d):
-            plane_copy(l, d).wait_send()
-            gather_copy(l, d).wait_send()
+            plane_copy(l, p, d).wait_send()
+            gather_copy(l, p, d).wait_send()
 
         @pl.loop(1, NZ)
         def _(d):
-            z_copy(l, d).wait_send()
+            z_copy(l, p, d).wait_send()
+
 
     def flat_rows(plane, i):
         return plane[i, 3 : 3 + TC].reshape(blk, CH)
-
-    def cot_rows(i):
-        return grad[rows_of(i)]
 
     def step_back(l):
         @pl.loop(0, NI)
@@ -498,8 +520,10 @@
             rows = rows_of(i)
             grad[rows] = grad[rows] + conv_rows(i)
 
+    ready(feat, place, edges)
     xp[0, :, 3 : 3 + TC] = nn(place[...], feat[...]).reshape(NI, TC, NS, CH)
     halo_start(0, xp.at[0])
+    ready(cot, dw, spread)
     grad[...] = nn(place[...], cot[...])
 
     @pl.loop(0, TAPS)
@@ -513,6 +537,7 @@
     halo_wait(0)
     assemble(0, xp.at[0], qa.at[0])
     convolve(qa.at[0], 0, False)
+    ready(up, down)
 
     def keep(i, new):
         xp[1, i, 3 : 3 + TC] = new.astype(F32).reshape(TC, NS, CH)
@@ -533,64 +558,114 @@
     def _(i):
         forward(1, xp.at[1], keep_out, i)
 
-    sums = backward_all(1, cot_rows)
+    early = branch_grads(1)
+    down_grads(1)
+    core_copy(1, 0).start()
+    sums = backward(1)
     halo_start(2, gx)
-    weight_grads(1)
+    to_plane(1, 0)
+    up_grads(1)
     tap_grads(1)
-    small_grads(1, sums)
-    core_copy(1).start()
-    out_ref[...] = tn(place[...], outq[...]).astype(BF16)
+    small_grads(1, early, sums)
+    core_copy(1, 1).start()
     halo_wait(2)
     assemble(2, gx, qg)
+    to_z(1, 0)
+    to_plane(1, 1)
     convolve(qg, 1, True)
     step_back(1)
-    to_plane(1)
-    sums = backward_all(0, cot_rows)
+    early = branch_grads(0)
+    down_grads(0)
+    core_copy(0, 0).start()
+    to_all(1, 0)
+    to_z(1, 1)
+    sums = backward(0)
     halo_start(3, gx)
-    to_z(1)
-    weight_grads(0)
-    to_all(1)
+    to_plane(0, 0)
+    up_grads(0)
+    to_sibling(1, 0)
     tap_grads(0)
-    small_grads(0, sums)
-    core_copy(0).start()
-    to_sibling(1)
+    small_grads(0, early, sums)
+    core_copy(0, 1).start()
+    to_all(1, 1)
     halo_wait(3)
     assemble(3, gx, qg)
-    to_plane(0)
+    to_z(0, 0)
+    to_plane(0, 1)
     convolve(qg, 0, True)
     step_back(0)
-    to_z(0)
+    to_sibling(1, 1)
+    to_all(0, 0)
+    to_z(0, 1)
+    out_ref[...] = tn(place[...], outq[...]).astype(BF16)
+    leave(0, out_ref, out_to).start()
     g = grad[...]
     high = g.astype(BF16)
     g = g - high.astype(F32)
     mid = g.astype(BF16)
     low = (g - mid.astype(F32)).astype(BF16)
     gfeat_ref[...] = tn(place[...], high) + (tn(place[...], mid) + tn(place[...], low))
-    to_all(0)
-    to_sibling(0)
+    leave(1, gfeat_ref, gfeat_to).start()
+    to_sibling(0, 0)
+    to_all(0, 1)
+    finish(1, 0)
+    leave(2, result0.at[1], result0_to.at[1]).start()
+    finish(1, 1)
+    leave(3, result1.at[1], result1_to.at[1]).start()
     for n in range(4):
         halo_done(n)
-    finish(1)
-    finish(0)
-
-
-def unpack(out_in, gfeat_in, result, out, gfeat, gtaps, gcbias, ggain, gshift, gup, gubias, gdown, gdbias, gscale, few):
-    out[...] = out_in[...]
-    gfeat[...] = gfeat_in[...]
+    to_sibling(0, 1)
+    finish(0, 0)
+    leave(4, result0.at[0], result0_to.at[0]).start()
+    finish(0, 1)
+    leave(5, result1.at[0], result1_to.at[0]).start()
+    leave(0, out_ref, out_to).wait()
+    leave(1, gfeat_ref, gfeat_to).wait()
+    leave(2, result0.at[1], result0_to.at[1]).wait()
+    leave(3, result1.at[1], result1_to.at[1]).wait()
+    leave(4, result0.at[0], result0_to.at[0]).wait()
+    leave(5, result1.at[0], result1_to.at[0]).wait()
+
+
+def unpack(out_in, gfeat_in, result0_in, result1_in,
+           out, gfeat, gtaps, gcbias, ggain, gshift, gup, gubias, gdown, gdbias, gscale,
+           few, result0, result1, ins):
+    copies = [
+        pltpu.make_async_copy(src, dst, ins.at[k])
+        for k, (src, dst) in enumerate(
+            ((result0_in, result0), (result1_in, result1), (gfeat_in, gfeat), (out_in, out))
+        )
+    ]
+    for copy in copies:
+        copy.start()
     upper = lax.broadcasted_iota(jnp.int32, (8, LANES), 0) < 4
+
+    def place_tile(l, ref, index, tile):
+        t, r = divmod(index, CH // 8)
+        ref[l, 8 * r : 8 * r + 8, LANES * t : LANES * t + LANES] = tile
+
+    copies[0].wait()
     for l in range(2):
-        for piece in range(96):
-            chunk, slot = divmod(piece, 3)
-            m, piece = divmod(piece, 48)
-            t, r = divmod(piece, 8)
-            value = result[l, chunk // CHUNKS, chunk % CHUNKS, 24 * slot : 24 * slot + 24].astype(F32)
-            (gup, gdown)[m][l, 24 * r : 24 * r + 24, LANES * t : LANES * t + LANES] = value
-        for k in range(CHUNKS):
-            pair = []
-            for chunk in (2 * k, 2 * k + 1):
-                v = result[l, chunk // CHUNKS, chunk % CHUNKS, BIG:].astype(F32)
-                pair.append(v + pltpu.roll(v, 4, 0))
-            few[8 * k : 8 * k + 8] = jnp.where(upper, pair[0], pair[1])
+        for chunk in range(2 * CHUNKS):
+            v = result0[l, chunk // CHUNKS, chunk % CHUNKS].astype(F32)
+            for slot in range(4):
+                place_tile(l, gdown, 4 * chunk + slot, v[8 * slot : 8 * slot + 8])
+    copies[1].wait()
+    for l in range(2):
+        pair = []
+        for chunk in range(2 * CHUNKS):
+            v = result1[l, chunk // CHUNKS, chunk % CHUNKS].astype(F32)
+            for slot in range(5):
+                index = 5 * chunk + slot
+                tile = v[8 * slot : 8 * slot + 8]
+                if index < CH // 8 * 6:
+                    place_tile(l, gup, index, tile)
+                else:
+                    place_tile(l, gdown, index - CH // 8 * 6 + DTILES, tile)
+            v = v[SMALL_AT:]
+            pair.append(v + pltpu.roll(v, 4, 0))
+            if chunk % 2:
+                few[4 * chunk - 4 : 4 * chunk + 4] = jnp.where(upper, pair[-2], pair[-1])
         for t in range(TAPS):
             gtaps[t, l : l + 1, :LANES] = few[t : t + 1]
             gtaps[t, l : l + 1, LANES:] = few[TAPS + t : TAPS + t + 1, :REST]
@@ -600,6 +675,8 @@
             ref[l : l + 1, LANES:] = few[at + 1 : at + 2, :REST]
         for t in range(6):
             gubias[l : l + 1, LANES * t : LANES * t + LANES] = few[ROW_UBIAS + t : ROW_UBIAS + t + 1]
+    copies[2].wait()
+    copies[3].wait()
 
 
 def on_device(features, cotangent, dw_kernel, conv_bias, ln_gain, ln_shift, up_weight, up_bias,
@@ -612,16 +689,30 @@
     dma = pltpu.SemaphoreType.DMA
     plane = (NI, TC + 6, NS, CH)
     wide = (NI + 6, WIDE, NS, LANES)
-    out, gfeat, result = pl.pallas_call(
+    hbm = pl.BlockSpec(memory_space=pltpu.HBM)
+    results = tuple(jax.ShapeDtypeStruct((depth, 2, CHUNKS, rows, LANES), BF16) for rows in PARTS)
+    out, gfeat, result0, result1 = pl.pallas_call(
         functools.partial(kernel, 1.0 / math.sqrt(pixel_total)),
         out_shape=(
             jax.ShapeDtypeStruct((PX, CH), BF16),
             jax.ShapeDtypeStruct((PX, CH), F32),
-            jax.ShapeDtypeStruct((depth, 2, CHUNKS, ROWS, LANES), BF16),
+            *results,
         ),
-        in_specs=[vmem] * 14,
-        out_specs=(vmem,) * 3,
+        in_specs=[hbm] * 3 + [vmem] * 3 + [hbm, vmem, hbm] + [vmem] * 2 + [hbm] * 3,
+        out_specs=(hbm,) * 4,
         scratch_shapes=[
+            pltpu.VMEM((PX, CH), BF16),
+            pltpu.VMEM((PX, CH), BF16),
+            pltpu.VMEM((TAPS, depth, CH), F32),
+            pltpu.VMEM((depth, CH, HID), BF16),
+            pltpu.VMEM((depth, CH, HID), BF16),
+            pltpu.VMEM(place.shape, BF16),
+            pltpu.VMEM(edges.shape, BF16),
+            pltpu.VMEM(spread.shape, BF16),
+            pltpu.VMEM((PX, CH), BF16),
+            pltpu.VMEM((PX, CH), F32),
+            *(pltpu.VMEM(v.shape, v.dtype) for v in results),
+            dma((8,)), dma((6,)),
             pltpu.VMEM((2, *plane), F32),
             pltpu.VMEM(plane, F32),
             pltpu.VMEM((2, *wide), F32),
@@ -643,21 +734,21 @@
             pltpu.VMEM((PX, CH), F32),
             pltpu.VMEM((PX, CH), BF16),
             pltpu.VMEM((2, 2, TAPS, NS, LANES), F32),
-            pltpu.VMEM((2, 2, CHUNKS, ROWS, LANES), F32),
-            pltpu.VMEM((2, CHUNKS, ROWS, LANES), F32),
-            pltpu.VMEM((2, CHUNKS, ROWS, LANES), BF16),
-            pltpu.VMEM((2, CHUNKS, ROWS, LANES), BF16),
-            pltpu.VMEM((2, NZ, ROWS, LANES), BF16),
+            *(pltpu.VMEM((2, 2, CHUNKS, rows, LANES), F32) for rows in PARTS),
+            *(pltpu.VMEM((2, CHUNKS, rows, LANES), F32) for rows in PARTS),
+            *(pltpu.VMEM((2, CHUNKS, rows, LANES), BF16) for rows in PARTS),
+            *(pltpu.VMEM((2, CHUNKS, rows, LANES), BF16) for rows in PARTS),
+            *(pltpu.VMEM((2, NZ, rows, LANES), BF16) for rows in PARTS),
             pltpu.VMEM((4, 2, 3, TR, CH), BF16),
             pltpu.VMEM((4, 2, 3, TC, CH), BF16),
             pltpu.VMEM((4, 2, 3, TR, CH), BF16),
             pltpu.VMEM((4, 6, 3, TC, CH), BF16),
             dma((4, 8)), dma((4, 8)),
-            dma((2,)), dma((2,)),
-            dma((2, CHUNKS)), dma((2, CHUNKS)),
-            dma((2, NZ)), dma((2, NZ)),
-            dma((2, CHUNKS)), dma((2, CHUNKS)),
-            dma((2, CHUNKS)), dma((2, CHUNKS)),
+            dma((4,)), dma((4,)),
+            dma((4, CHUNKS)), dma((4, CHUNKS)),
+            dma((4, NZ)), dma((4, NZ)),
+            dma((4, CHUNKS)), dma((4, CHUNKS)),
+            dma((4, CHUNKS)), dma((4, CHUNKS)),
         ],
         compiler_params=pltpu.CompilerParams(
             collective_id=0, has_side_effects=True, vmem_limit_bytes=56 * 2**20
@@ -676,11 +767,15 @@
             jax.ShapeDtypeStruct((TAPS, depth, CH), F32),
             vector, vector, vector, weight, jax.ShapeDtypeStruct((depth, HID), F32), weight, vector, vector,
         ),
-        in_specs=[vmem] * 3,
+        in_specs=[hbm] * 4,
         out_specs=(vmem,) * 11,
-        scratch_shapes=[pltpu.VMEM((LANES, LANES), F32)],
-        compiler_params=pltpu.CompilerParams(vmem_limit_bytes=24 * 2**20),
-    )(out, gfeat, result)
+        scratch_shapes=[
+            pltpu.VMEM((LANES, LANES), F32),
+            *(pltpu.VMEM(v.shape, v.dtype) for v in results),
+            dma((4,)),
+        ],
+        compiler_params=pltpu.CompilerParams(vmem_limit_bytes=56 * 2**20),
+    )(out, gfeat, result0, result1)
     return (
         out.reshape(1, TR, TC, CH),
         gfeat.reshape(1, TR, TC, CH),

time: 94.4 us -> 84.9 us (0.90)
  Pallas kernels: 90.2 us -> 84.1 us
  local copies, waits for them, and re-layouts: 3.3 us -> 0 us
    pallas_call x1, Pallas kernels: 88.5 us -> 80.8 us  [on_device(): pl.pallas_call(functools.partial(kernel, 1.0 / math.sqrt(pixel_total)), o...]
    unnamed x6 -> x0, local copies, waits for them, and re-layouts: 3.3 us -> none
    pallas_call x1, Pallas kernels: 1.74 us -> 3.26 us  [on_device(): pl.pallas_call(unpack, out_shape=(jax.ShapeDtypeStruct((PX, CH), BF16), j...]
where the time goes in v3:
time: 84.9 us; the launch traced here: 84.7 us
  Pallas kernels  84.1 us (99%)
    pallas_call x1, Pallas kernels, on_device(): pl.pallas_call(functools.partial(kernel, 1.0 / math.sqrt(pixel_total)), o...  80.8 us
    pallas_call x1, Pallas kernels, on_device(): pl.pallas_call(unpack, out_shape=(jax.ShapeDtypeStruct((PX, CH), BF16), j...  3.26 us

profile of v3, /device:TPU:1, one launch (start us, length us, event | category | flops | bytes accessed | tf_op | source)
XLA Modules:
  0.0 84.7 jit_solution(4384805391084567269)
XLA Ops:
  0.6 80.8 %shard_map.221 = (bf16[512,192]{1,0:T(8,128)(2,1)}, f32[512,192]{1,0:T(8,128)}, bf16[2,2,16,32,128]{4,3,2,1,0:T(8,128)(2,1)}, bf16[2,2,16,48,128]{4,3,2,1,0:T(8,128)(2,1)}) custom-call(bf16[512,192]{1,0:T(8,128)(2,1)} %bitcast.13, bf16[512,192]{1,0:T(8,128)(2,1)} %bitcast.14, f32[49,2,192]{2,1,0:T(2,128)} %bitcast.15, f32[2,192]{1,0:T(2,128)} %cbias.1, ...), custom_call_target="tpu_custom_call" | custom-call | tf_op jit(solution)/shard_map/pallas_call | solution.py:694
  81.5 3.3 %shard_map.222 = (bf16[512,192]{1,0:T(8,128)(2,1)}, f32[512,192]{1,0:T(8,128)}, f32[49,2,192]{2,1,0:T(2,128)}, f32[2,192]{1,0:T(2,128)}, f32[2,192]{1,0:T(2,128)...) custom-call(bf16[512,192]{1,0:T(8,128)(2,1)} %get-tuple-element.26.o, ...), custom_call_target="tpu_custom_call" | custom-call | tf_op jit(solution)/shard_map/pallas_call | solution.py:762

commit v4 on v3

--- a/solution.py
+++ b/solution.py
@@ -28,7 +28,7 @@
 WIDE = (TC + 2 * MARGIN) + (TC // 2 + 2 * MARGIN)
 PARTS = (32, 48)
 DTILES = 128
-SMALL_AT = 40
+USED = 40
 CHUNKS = 16
 NZ = 8
 HALOS = ((-1, -1), (-1, 0), (-1, 1), (1, -1), (1, 0), (1, 1), (0, -1), (0, 1))
@@ -74,13 +74,13 @@
 def kernel(
     factor,
     feat_in, cot_in, dw_in, cbias, gain, shift, up_in, ubias, down_in, dbias, scale, place_in, edges_in, spread_in,
-    out_to, gfeat_to, result0_to, result1_to,
-    feat, cot, dw, up, down, place, edges, spread, out_ref, gfeat_ref, result0, result1, ins, outs,
+    out_to, gfeat_to, result0_to, result1_to, result2_to,
+    feat, cot, dw, up, down, place, edges, spread, out_ref, gfeat_ref, result0, result1, result2, ins, outs,
     xp, gx, qa, qg, cbuf, conv, unit, inv, normed, act, slope, branch, gbr, gpre, gcp, tq, taps, small,
     grad, outq, wexp,
     pay0, pay1, core0, core1, sbuf0, sbuf1, rbuf0, rbuf1, zbuf0, zbuf1,
-    csend, rsend, crecv, rrecv,
-    hs, hr, cs, cr, xs, xr, zs, zr, gs, gr, ls, lr,
+    few, fewr, fewz, csend, rsend, crecv, rrecv,
+    hs, hr, cs, cr, xs, xr, zs, zr, gs, gr, ls, lr, fs, fr,
 ):
     yh = lax.axis_index("slide")
     ty = lax.axis_index("ty")
@@ -98,6 +98,11 @@
         pl_ = lax.rem(yl + lax.rem(d, 2), 2)
         return py * 4 + ph * 2 + pl_, (ph, py, z * 4 + pl_ * 2 + core)
 
+    def column_peer(e):
+        pz = lax.rem(z + lax.div(e, 2), NZ)
+        pc = lax.rem(core + lax.rem(e, 2), 2)
+        return pz * 2 + pc, (yh, ty, pz * 4 + yl * 2 + pc)
+
     def z_peer(d):
         pz = lax.rem(z + d, NZ)
         return pz, (yh, ty, pz * 4 + yl * 2 + core)
@@ -109,15 +114,13 @@
 
     for dy, dx in HALOS:
         greet((yh, lax.rem(ty + dy + 4, 4), lax.rem(tx + dx + 32, 32)))
-    greet(sibling)
-
     @pl.loop(1, CHUNKS)
     def _(d):
         greet(plane_peer(d)[1])
 
-    @pl.loop(1, NZ)
-    def _(d):
-        greet(z_peer(d)[1])
+    @pl.loop(1, 2 * NZ)
+    def _(e):
+        greet(column_peer(e)[1])
 
     arrivals = {}
     loads = ((feat_in, feat), (place_in, place), (edges_in, edges), (cot_in, cot), (dw_in, dw), (spread_in, spread),
@@ -161,7 +164,7 @@
             csend[n, 0, c] = plane[:, 3 + c].reshape(TR, CH).astype(BF16)
             csend[n, 1, c] = plane[:, TC + c].reshape(TR, CH).astype(BF16)
         if n == 0:
-            pl.semaphore_wait(barrier, 8 + 1 + CHUNKS - 1 + NZ - 1)
+            pl.semaphore_wait(barrier, 8 + CHUNKS - 1 + 2 * NZ - 1)
         for dy, dx in HALOS:
 
             @pl.when(there(dy, dx))
@@ -289,14 +292,20 @@
 
         return lax.fori_loop(0, NI, body, (jnp.zeros((8, CH), F32),) * 2)
 
+    def pre_grads(l):
+        def body(i, total):
+            rows = rows_of(i)
+            gp = (nn(gbr[rows], down[l]) * slope[l, rows]).astype(BF16)
+            gpre[rows] = gp
+            return total + fold(gp.astype(F32))
+
+        return lax.fori_loop(0, NI, body, jnp.zeros((8, HID), F32))
+
     def backward(l):
         def body(i, sums):
             rows = rows_of(i)
-            s_gain, s_shift, s_ubias, s_cbias = sums
-            gp = (nn(gbr[rows], down[l]) * slope[l, rows]).astype(BF16)
-            gpre[rows] = gp
-            s_ubias = s_ubias + fold(gp.astype(F32))
-            gn = nt(gp, up[l])
+            s_gain, s_shift, s_cbias = sums
+            gn = nt(gpre[rows], up[l])
             u = unit[l, rows]
             s_gain = s_gain + fold(gn * u)
             s_shift = s_shift + fold(gn)
@@ -309,10 +318,10 @@
             half = blk // 2
             gcp[i, TC:, :, :REST] = gc[:half, LANES:].reshape(TC // 2, NS, REST)
             gcp[i, TC:, :, REST:] = gc[half:, LANES:].reshape(TC // 2, NS, REST)
-            return s_gain, s_shift, s_ubias, s_cbias
+            return s_gain, s_shift, s_cbias
 
         zero = jnp.zeros((8, CH), F32)
-        return lax.fori_loop(0, NI, body, (zero, zero, jnp.zeros((8, HID), F32), zero))
+        return lax.fori_loop(0, NI, body, (zero, zero, zero))
 
     def put(l, index, tile, tiles, pay):
         chunk, slot = divmod(index, tiles)
@@ -359,9 +368,9 @@
                 for r in range(SPAN):
                     taps[part, r * SPAN + j] = sums[r]
 
-    def small_grads(l, early, sums):
+    def small_grads(l, early, s_ubias, sums):
         s_dbias, s_scale = early
-        s_gain, s_shift, s_ubias, s_cbias = sums
+        s_gain, s_shift, s_cbias = sums
         small[...] = jnp.zeros((LANES, LANES), F32)
         small[:TAPS] = jnp.sum(taps[0], axis=1)
         rest = jnp.sum(taps[1], axis=1)
@@ -374,22 +383,7 @@
         v = jnp.sum(s_ubias, axis=0, keepdims=True)
         for t in range(6):
             small[ROW_UBIAS + t : ROW_UBIAS + t + 1] = v[:, LANES * t : LANES * t + LANES]
-        upper = lax.broadcasted_iota(jnp.int32, (8, LANES), 0) < 4
-        for k in range(2 * CHUNKS):
-            v = small[8 * (k // 2) : 8 * (k // 2) + 8]
-            if k % 2:
-                v = pltpu.roll(v, 4, 0)
-            pay1[l, k // CHUNKS, k % CHUNKS, SMALL_AT:] = jnp.where(upper, v, 0.0)
-
-    upper = lax.broadcasted_iota(jnp.int32, (8, LANES), 0) < 4
-
-    def rounded(v, part):
-        if part == 0:
-            return v.astype(BF16)
-        s = v[SMALL_AT:]
-        s = s + pltpu.roll(s, 4, 0)
-        high = s.astype(BF16).astype(F32)
-        return jnp.concatenate([v[:SMALL_AT], jnp.where(upper, high, s - high)], axis=0).astype(BF16)
+        few[l] = small[...].reshape(CHUNKS, 8, LANES)
 
     pays, cores, sbufs, rbufs, zbufs = (pay0, pay1), (core0, core1), (sbuf0, sbuf1), (rbuf0, rbuf1), (zbuf0, zbuf1)
     results = (result0, result1)
@@ -453,7 +447,7 @@
             d = lax.rem(k + 1, CHUNKS)
             index, _ = plane_peer(d)
             v = pays[p][l, core, index] + cores[p][l, index]
-            sbufs[p][l, index] = rounded(v, p)
+            sbufs[p][l, index] = v.astype(BF16)
 
             @pl.when(d > 0)
             def _():
@@ -465,7 +459,7 @@
             plane_copy(l, p, d).wait_recv()
 
         v = lax.fori_loop(1, CHUNKS, lambda d, v: v + rbufs[p][l, d].astype(F32), sbufs[p][l, me].astype(F32))
-        zbufs[p][l, z] = rounded(v, p)
+        zbufs[p][l, z] = v.astype(BF16)
 
         @pl.loop(1, NZ)
         def _(d):
@@ -479,7 +473,7 @@
         v = zbufs[p][l, 0].astype(F32)
         for k in range(1, NZ):
             v = v + zbufs[p][l, k].astype(F32)
-        results[p][l, core, me] = rounded(v * factor, p)
+        results[p][l, core, me] = (v * factor).astype(BF16)
 
         @pl.loop(1, CHUNKS)
         def _(d):
@@ -511,6 +505,70 @@
             z_copy(l, p, d).wait_send()
 
 
+    def few_copy(l, stage, d):
+        if stage == 0:
+            index, device = plane_peer(d)
+            src, dst, slot = few.at[l, index], fewr.at[l, d], d
+        elif stage == 1:
+            device = column_peer(d)[1]
+            slot = z * 2 + core
+            src = dst = fewz.at[l, slot]
+        else:
+            device, slot = plane_peer(d)[1], me
+            src = dst = result2.at[l, slot]
+        return pltpu.make_async_remote_copy(
+            src_ref=src, dst_ref=dst, send_sem=fs.at[3 * l + stage, d], recv_sem=fr.at[3 * l + stage, slot],
+            device_id=device, device_id_type=MESH,
+        )
+
+    def few_arrival(l, stage, d):
+        if stage == 0:
+            return few_copy(l, 0, d)
+        if stage == 1:
+            slot, device = column_peer(d)
+            ref = fewz.at[l, slot]
+        else:
+            slot, device = plane_peer(d)
+            ref = result2.at[l, slot]
+        return pltpu.make_async_remote_copy(
+            src_ref=ref, dst_ref=ref, send_sem=fs.at[3 * l + stage, d], recv_sem=fr.at[3 * l + stage, slot],
+            device_id=device, device_id_type=MESH,
+        )
+
+    def few_send(l, stage):
+        @pl.loop(1, CHUNKS)
+        def _(d):
+            few_copy(l, stage, d).start()
+
+    def few_wait(l, stage):
+        @pl.loop(1, CHUNKS)
+        def _(d):
+            few_arrival(l, stage, d).wait_recv()
+
+    def few_column(l):
+        few_wait(l, 0)
+        v = few[l, me]
+        for d in range(1, CHUNKS):
+            v = v + fewr[l, d]
+        fewz[l, z * 2 + core] = v
+        few_send(l, 1)
+
+    def few_plane(l):
+        few_wait(l, 1)
+        v = fewz[l, 0]
+        for k in range(1, 2 * NZ):
+            v = v + fewz[l, k]
+        result2[l, me] = v * factor
+        few_send(l, 2)
+
+    def few_finish(l):
+        few_wait(l, 2)
+
+        @pl.loop(1, CHUNKS)
+        def _(d):
+            for stage in range(3):
+                few_copy(l, stage, d).wait_send()
+
     def flat_rows(plane, i):
         return plane[i, 3 : 3 + TC].reshape(blk, CH)
 
@@ -523,6 +581,9 @@
     ready(feat, place, edges)
     xp[0, :, 3 : 3 + TC] = nn(place[...], feat[...]).reshape(NI, TC, NS, CH)
     halo_start(0, xp.at[0])
+    for l in range(2):
+        for k in range(2 * CHUNKS):
+            pay1[l, k // CHUNKS, k % CHUNKS, USED:] = jnp.zeros((8, LANES), F32)
     ready(cot, dw, spread)
     grad[...] = nn(place[...], cot[...])
 
@@ -558,87 +619,98 @@
     def _(i):
         forward(1, xp.at[1], keep_out, i)
 
+    def leave_all(l):
+        return [leave(3 * l + k, v.at[l], to.at[l]) for k, (v, to) in enumerate(
+            ((result0, result0_to), (result1, result1_to), (result2, result2_to)))]
+
     early = branch_grads(1)
     down_grads(1)
     core_copy(1, 0).start()
+    s_ubias = pre_grads(1)
+    up_grads(1)
+    core_copy(1, 1).start()
     sums = backward(1)
     halo_start(2, gx)
     to_plane(1, 0)
-    up_grads(1)
     tap_grads(1)
-    small_grads(1, early, sums)
-    core_copy(1, 1).start()
+    to_plane(1, 1)
+    small_grads(1, early, s_ubias, sums)
+    few_send(1, 0)
     halo_wait(2)
     assemble(2, gx, qg)
     to_z(1, 0)
-    to_plane(1, 1)
     convolve(qg, 1, True)
     step_back(1)
     early = branch_grads(0)
     down_grads(0)
     core_copy(0, 0).start()
-    to_all(1, 0)
     to_z(1, 1)
+    s_ubias = pre_grads(0)
+    up_grads(0)
+    core_copy(0, 1).start()
+    few_column(1)
+    to_plane(0, 0)
     sums = backward(0)
     halo_start(3, gx)
-    to_plane(0, 0)
-    up_grads(0)
-    to_sibling(1, 0)
+    to_plane(0, 1)
+    to_all(1, 0)
     tap_grads(0)
-    small_grads(0, early, sums)
-    core_copy(0, 1).start()
-    to_all(1, 1)
+    small_grads(0, early, s_ubias, sums)
+    few_send(0, 0)
+    few_plane(1)
     halo_wait(3)
     assemble(3, gx, qg)
     to_z(0, 0)
-    to_plane(0, 1)
+    to_all(1, 1)
     convolve(qg, 0, True)
     step_back(0)
-    to_sibling(1, 1)
-    to_all(0, 0)
     to_z(0, 1)
-    out_ref[...] = tn(place[...], outq[...]).astype(BF16)
-    leave(0, out_ref, out_to).start()
+    few_column(0)
+    to_sibling(1, 0)
     g = grad[...]
     high = g.astype(BF16)
     g = g - high.astype(F32)
     mid = g.astype(BF16)
     low = (g - mid.astype(F32)).astype(BF16)
     gfeat_ref[...] = tn(place[...], high) + (tn(place[...], mid) + tn(place[...], low))
-    leave(1, gfeat_ref, gfeat_to).start()
-    to_sibling(0, 0)
+    leave(6, gfeat_ref, gfeat_to).start()
+    to_all(0, 0)
+    few_plane(0)
+    to_sibling(1, 1)
+    out_ref[...] = tn(place[...], outq[...]).astype(BF16)
+    leave(7, out_ref, out_to).start()
     to_all(0, 1)
-    finish(1, 0)
-    leave(2, result0.at[1], result0_to.at[1]).start()
-    finish(1, 1)
-    leave(3, result1.at[1], result1_to.at[1]).start()
     for n in range(4):
         halo_done(n)
+    to_sibling(0, 0)
+    for p in range(2):
+        finish(1, p)
+    few_finish(1)
+    for copy in leave_all(1):
+        copy.start()
+    few_finish(0)
     to_sibling(0, 1)
-    finish(0, 0)
-    leave(4, result0.at[0], result0_to.at[0]).start()
-    finish(0, 1)
-    leave(5, result1.at[0], result1_to.at[0]).start()
-    leave(0, out_ref, out_to).wait()
-    leave(1, gfeat_ref, gfeat_to).wait()
-    leave(2, result0.at[1], result0_to.at[1]).wait()
-    leave(3, result1.at[1], result1_to.at[1]).wait()
-    leave(4, result0.at[0], result0_to.at[0]).wait()
-    leave(5, result1.at[0], result1_to.at[0]).wait()
-
-
-def unpack(out_in, gfeat_in, result0_in, result1_in,
+    for p in range(2):
+        finish(0, p)
+    for copy in leave_all(0):
+        copy.start()
+    for copy in leave_all(0) + leave_all(1):
+        copy.wait()
+    leave(6, gfeat_ref, gfeat_to).wait()
+    leave(7, out_ref, out_to).wait()
+
+
+def unpack(out_in, gfeat_in, result0_in, result1_in, result2_in,
            out, gfeat, gtaps, gcbias, ggain, gshift, gup, gubias, gdown, gdbias, gscale,
-           few, result0, result1, ins):
+           result0, result1, result2, ins):
     copies = [
         pltpu.make_async_copy(src, dst, ins.at[k])
         for k, (src, dst) in enumerate(
-            ((result0_in, result0), (result1_in, result1), (gfeat_in, gfeat), (out_in, out))
+            ((result0_in, result0), (result1_in, result1), (result2_in, result2), (gfeat_in, gfeat), (out_in, out))
         )
     ]
     for copy in copies:
         copy.start()
-    upper = lax.broadcasted_iota(jnp.int32, (8, LANES), 0) < 4
 
     def place_tile(l, ref, index, tile):
         t, r = divmod(index, CH // 8)
@@ -652,7 +724,6 @@
                 place_tile(l, gdown, 4 * chunk + slot, v[8 * slot : 8 * slot + 8])
     copies[1].wait()
     for l in range(2):
-        pair = []
         for chunk in range(2 * CHUNKS):
             v = result1[l, chunk // CHUNKS, chunk % CHUNKS].astype(F32)
             for slot in range(5):
@@ -662,10 +733,9 @@
                     place_tile(l, gup, index, tile)
                 else:
                     place_tile(l, gdown, index - CH // 8 * 6 + DTILES, tile)
-            v = v[SMALL_AT:]
-            pair.append(v + pltpu.roll(v, 4, 0))
-            if chunk % 2:
-                few[4 * chunk - 4 : 4 * chunk + 4] = jnp.where(upper, pair[-2], pair[-1])
+    copies[2].wait()
+    for l in range(2):
+        few = result2[l].reshape(LANES, LANES)
         for t in range(TAPS):
             gtaps[t, l : l + 1, :LANES] = few[t : t + 1]
             gtaps[t, l : l + 1, LANES:] = few[TAPS + t : TAPS + t + 1, :REST]
@@ -675,8 +745,8 @@
             ref[l : l + 1, LANES:] = few[at + 1 : at + 2, :REST]
         for t in range(6):
             gubias[l : l + 1, LANES * t : LANES * t + LANES] = few[ROW_UBIAS + t : ROW_UBIAS + t + 1]
-    copies[2].wait()
     copies[3].wait()
+    copies[4].wait()
 
 
 def on_device(features, cotangent, dw_kernel, conv_bias, ln_gain, ln_shift, up_weight, up_bias,
@@ -690,8 +760,10 @@
     plane = (NI, TC + 6, NS, CH)
     wide = (NI + 6, WIDE, NS, LANES)
     hbm = pl.BlockSpec(memory_space=pltpu.HBM)
-    results = tuple(jax.ShapeDtypeStruct((depth, 2, CHUNKS, rows, LANES), BF16) for rows in PARTS)
-    out, gfeat, result0, result1 = pl.pallas_call(
+    results = tuple(jax.ShapeDtypeStruct((depth, 2, CHUNKS, rows, LANES), BF16) for rows in PARTS) + (
+        jax.ShapeDtypeStruct((depth, CHUNKS, 8, LANES), F32),
+    )
+    out, gfeat, result0, result1, result2 = pl.pallas_call(
         functools.partial(kernel, 1.0 / math.sqrt(pixel_total)),
         out_shape=(
             jax.ShapeDtypeStruct((PX, CH), BF16),
@@ -699,7 +771,7 @@
             *results,
         ),
         in_specs=[hbm] * 3 + [vmem] * 3 + [hbm, vmem, hbm] + [vmem] * 2 + [hbm] * 3,
-        out_specs=(hbm,) * 4,
+        out_specs=(hbm,) * 5,
         scratch_shapes=[
             pltpu.VMEM((PX, CH), BF16),
             pltpu.VMEM((PX, CH), BF16),
@@ -712,7 +784,7 @@
             pltpu.VMEM((PX, CH), BF16),
             pltpu.VMEM((PX, CH), F32),
             *(pltpu.VMEM(v.shape, v.dtype) for v in results),
-            dma((8,)), dma((6,)),
+            dma((8,)), dma((8,)),
             pltpu.VMEM((2, *plane), F32),
             pltpu.VMEM(plane, F32),
             pltpu.VMEM((2, *wide), F32),
@@ -739,6 +811,9 @@
             *(pltpu.VMEM((2, CHUNKS, rows, LANES), BF16) for rows in PARTS),
             *(pltpu.VMEM((2, CHUNKS, rows, LANES), BF16) for rows in PARTS),
             *(pltpu.VMEM((2, NZ, rows, LANES), BF16) for rows in PARTS),
+            pltpu.VMEM((2, CHUNKS, 8, LANES), F32),
+            pltpu.VMEM((2, CHUNKS, 8, LANES), F32),
+            pltpu.VMEM((2, 2 * NZ, 8, LANES), F32),
             pltpu.VMEM((4, 2, 3, TR, CH), BF16),
             pltpu.VMEM((4, 2, 3, TC, CH), BF16),
             pltpu.VMEM((4, 2, 3, TR, CH), BF16),
@@ -749,6 +824,7 @@
             dma((4, NZ)), dma((4, NZ)),
             dma((4, CHUNKS)), dma((4, CHUNKS)),
             dma((4, CHUNKS)), dma((4, CHUNKS)),
+            dma((6, CHUNKS)), dma((6, CHUNKS)),
         ],
         compiler_params=pltpu.CompilerParams(
             collective_id=0, has_side_effects=True, vmem_limit_bytes=56 * 2**20
@@ -767,15 +843,14 @@
             jax.ShapeDtypeStruct((TAPS, depth, CH), F32),
             vector, vector, vector, weight, jax.ShapeDtypeStruct((depth, HID), F32), weight, vector, vector,
         ),
-        in_specs=[hbm] * 4,
+        in_specs=[hbm] * 5,
         out_specs=(vmem,) * 11,
         scratch_shapes=[
-            pltpu.VMEM((LANES, LANES), F32),
             *(pltpu.VMEM(v.shape, v.dtype) for v in results),
-            dma((4,)),
+            dma((5,)),
         ],
         compiler_params=pltpu.CompilerParams(vmem_limit_bytes=56 * 2**20),
-    )(out, gfeat, result0, result1)
+    )(out, gfeat, result0, result1, result2)
     return (
         out.reshape(1, TR, TC, CH),
         gfeat.reshape(1, TR, TC, CH),

time: 84.9 us -> 89.3 us (1.052)
  Pallas kernels: 84.1 us -> 88.5 us
    pallas_call x1, Pallas kernels: 80.8 us -> 85.2 us  [on_device(): pl.pallas_call(functools.partial(kernel, 1.0 / math.sqrt(pixel_total)), o...]
where the time goes in v4:
time: 89.3 us; the launch traced here: 89.2 us
  Pallas kernels  88.5 us (99%)
    pallas_call x1, Pallas kernels, on_device(): pl.pallas_call(functools.partial(kernel, 1.0 / math.sqrt(pixel_total)), o...  85.2 us
    pallas_call x1, Pallas kernels, on_device(): pl.pallas_call(unpack, out_shape=(jax.ShapeDtypeStruct((PX, CH), BF16), j...  3.3 us

profile of v4, /device:TPU:1, one launch (start us, length us, event | category | flops | bytes accessed | tf_op | source)
XLA Modules:
  0.0 89.2 jit_solution(13343722734430613728)
XLA Ops:
  0.6 85.2 %shard_map.221 = (bf16[512,192]{1,0:T(8,128)(2,1)}, f32[512,192]{1,0:T(8,128)}, bf16[2,2,16,32,128]{4,3,2,1,0:T(8,128)(2,1)}, bf16[2,2,16,48,128]{4,3,2,1,0:T(8,128)(2,1)}, f32[2,16,8,128]{3,2,1,0:T(8,128)}) custom-call(bf16[512,192]{1,0:T(8,128)(2,1)} %bitcast.13, bf16[512,192]{1,0:T(8,128)(2,1)} %bitcast.14, f32[49,2,192]{2,1,0:T(2,128)} %bitcast.15, ...), custom_call_target="tpu_custom_call" | custom-call | tf_op jit(solution)/shard_map/pallas_call | solution.py:766
  85.8 3.3 %shard_map.222 = (bf16[512,192]{1,0:T(8,128)(2,1)}, f32[512,192]{1,0:T(8,128)}, f32[49,2,192]{2,1,0:T(2,128)}, f32[2,192]{1,0:T(2,128)}, f32[2,192]{1,0:T(2,128)...) custom-call(bf16[512,192]{1,0:T(8,128)(2,1)} %get-tuple-element.27.o, ...), custom_call_target="tpu_custom_call" | custom-call | tf_op jit(solution)/shard_map/pallas_call | solution.py:838

commit v5 on v3

--- a/solution.py
+++ b/solution.py
@@ -26,9 +26,9 @@
 REST = CH - LANES
 PACK = TC + TC // 2
 WIDE = (TC + 2 * MARGIN) + (TC // 2 + 2 * MARGIN)
-PARTS = (32, 48)
-DTILES = 128
-SMALL_AT = 40
+PARTS = (64, 16)
+TILES = CH // 8 * (HID // LANES)
+SMALL_AT = 8
 CHUNKS = 16
 NZ = 8
 HALOS = ((-1, -1), (-1, 0), (-1, 1), (1, -1), (1, 0), (1, 1), (0, -1), (0, 1))
@@ -76,7 +76,7 @@
     feat_in, cot_in, dw_in, cbias, gain, shift, up_in, ubias, down_in, dbias, scale, place_in, edges_in, spread_in,
     out_to, gfeat_to, result0_to, result1_to,
     feat, cot, dw, up, down, place, edges, spread, out_ref, gfeat_ref, result0, result1, ins, outs,
-    xp, gx, qa, qg, cbuf, conv, unit, inv, normed, act, slope, branch, gbr, gpre, gcp, tq, taps, small,
+    xp, gx, qa, qg, cbuf, convs, unit, inv, normed, act, slope, branch, gbr, gpre, gcp, tq, taps, small,
     grad, outq, wexp,
     pay0, pay1, core0, core1, sbuf0, sbuf1, rbuf0, rbuf1, zbuf0, zbuf1,
     csend, rsend, crecv, rrecv,
@@ -244,6 +244,7 @@
 
     def conv_rows(i):
         half = TC * NS // 2
+        conv = convs.at[i]
         conv[:, :LANES] = cbuf[i, :TC].reshape(TC * NS, LANES)
         rest = cbuf[i, TC:].reshape(half, LANES)
         conv[:half, LANES:] = rest[:, :REST]
@@ -287,16 +288,22 @@
             gbr[rows] = gb
             return sums[0] + fold(gb.astype(F32)), sums[1] + fold(g * branch[l, rows])
 
-        return lax.fori_loop(0, NI, body, (jnp.zeros((8, CH), F32),) * 2)
+        return lax.fori_loop(0, NI, body, (jnp.zeros((8, CH), F32),) * 2, unroll=True)
+
+    def pre_grads(l):
+        def body(i, total):
+            rows = rows_of(i)
+            gp = (nn(gbr[rows], down[l]) * slope[l, rows]).astype(BF16)
+            gpre[rows] = gp
+            return total + fold(gp.astype(F32))
+
+        return lax.fori_loop(0, NI, body, jnp.zeros((8, HID), F32), unroll=True)
 
     def backward(l):
         def body(i, sums):
             rows = rows_of(i)
-            s_gain, s_shift, s_ubias, s_cbias = sums
-            gp = (nn(gbr[rows], down[l]) * slope[l, rows]).astype(BF16)
-            gpre[rows] = gp
-            s_ubias = s_ubias + fold(gp.astype(F32))
-            gn = nt(gp, up[l])
+            s_gain, s_shift, s_cbias = sums
+            gn = nt(gpre[rows], up[l])
             u = unit[l, rows]
             s_gain = s_gain + fold(gn * u)
             s_shift = s_shift + fold(gn)
@@ -309,14 +316,18 @@
             half = blk // 2
             gcp[i, TC:, :, :REST] = gc[:half, LANES:].reshape(TC // 2, NS, REST)
             gcp[i, TC:, :, REST:] = gc[half:, LANES:].reshape(TC // 2, NS, REST)
-            return s_gain, s_shift, s_ubias, s_cbias
+            return s_gain, s_shift, s_cbias
 
         zero = jnp.zeros((8, CH), F32)
-        return lax.fori_loop(0, NI, body, (zero, zero, jnp.zeros((8, HID), F32), zero))
-
-    def put(l, index, tile, tiles, pay):
-        chunk, slot = divmod(index, tiles)
-        pay[l, chunk // CHUNKS, chunk % CHUNKS, 8 * slot : 8 * slot + 8] = tile
+        return lax.fori_loop(0, NI, body, (zero, zero, zero), unroll=True)
+
+    def put(l, index, tile):
+        if index < 256:
+            chunk, slot = divmod(index, 8)
+            pay0[l, chunk // CHUNKS, chunk % CHUNKS, 8 * slot : 8 * slot + 8] = tile
+        else:
+            chunk = index - 256
+            pay1[l, chunk // CHUNKS, chunk % CHUNKS, :8] = tile
 
     def weight_tiles(a, b, store):
         for t in range(3):
@@ -326,16 +337,10 @@
                     store((2 * t + v) * (CH // 8) + r, part[8 * r : 8 * r + 8, LANES * v : LANES * v + LANES])
 
     def down_grads(l):
-        def store(index, tile):
-            if index < DTILES:
-                put(l, index, tile, 4, pay0)
-            else:
-                put(l, index + CH // 8 * 6 - DTILES, tile, 5, pay1)
-
-        weight_tiles(gbr, act.at[l], store)
+        weight_tiles(gbr, act.at[l], lambda index, tile: put(l, index, tile))
 
     def up_grads(l):
-        weight_tiles(normed.at[l], gpre, lambda index, tile: put(l, index, tile, 5, pay1))
+        weight_tiles(normed.at[l], gpre, lambda index, tile: put(l, TILES + index, tile))
 
     def tap_grads(l):
         for part, (cols, base, first) in enumerate(((TC, 0, 0), (TC // 2, TC + 6, TC))):
@@ -359,9 +364,9 @@
                 for r in range(SPAN):
                     taps[part, r * SPAN + j] = sums[r]
 
-    def small_grads(l, early, sums):
+    def small_grads(l, early, s_ubias, sums):
         s_dbias, s_scale = early
-        s_gain, s_shift, s_ubias, s_cbias = sums
+        s_gain, s_shift, s_cbias = sums
         small[...] = jnp.zeros((LANES, LANES), F32)
         small[:TAPS] = jnp.sum(taps[0], axis=1)
         rest = jnp.sum(taps[1], axis=1)
@@ -542,7 +547,7 @@
     def keep(i, new):
         xp[1, i, 3 : 3 + TC] = new.astype(F32).reshape(TC, NS, CH)
 
-    @pl.loop(0, NI)
+    @pl.loop(0, NI, unroll=2)
     def _(i):
         forward(0, xp.at[0], keep, i)
 
@@ -554,38 +559,43 @@
     def keep_out(i, new):
         outq[rows_of(i)] = new
 
-    @pl.loop(0, NI)
+    @pl.loop(0, NI, unroll=2)
     def _(i):
         forward(1, xp.at[1], keep_out, i)
 
+    def leave_all(l):
+        return [leave(2 * l + k, v.at[l], to.at[l]) for k, (v, to) in enumerate(
+            ((result0, result0_to), (result1, result1_to)))]
+
     early = branch_grads(1)
+    s_ubias = pre_grads(1)
     down_grads(1)
+    up_grads(1)
     core_copy(1, 0).start()
     sums = backward(1)
     halo_start(2, gx)
     to_plane(1, 0)
-    up_grads(1)
     tap_grads(1)
-    small_grads(1, early, sums)
+    small_grads(1, early, s_ubias, sums)
     core_copy(1, 1).start()
     halo_wait(2)
     assemble(2, gx, qg)
-    to_z(1, 0)
     to_plane(1, 1)
     convolve(qg, 1, True)
+    to_z(1, 0)
     step_back(1)
     early = branch_grads(0)
+    s_ubias = pre_grads(0)
     down_grads(0)
+    up_grads(0)
     core_copy(0, 0).start()
-    to_all(1, 0)
     to_z(1, 1)
     sums = backward(0)
     halo_start(3, gx)
     to_plane(0, 0)
-    up_grads(0)
-    to_sibling(1, 0)
+    to_all(1, 0)
     tap_grads(0)
-    small_grads(0, early, sums)
+    small_grads(0, early, s_ubias, sums)
     core_copy(0, 1).start()
     to_all(1, 1)
     halo_wait(3)
@@ -594,37 +604,36 @@
     to_plane(0, 1)
     convolve(qg, 0, True)
     step_back(0)
-    to_sibling(1, 1)
+    to_sibling(1, 0)
     to_all(0, 0)
     to_z(0, 1)
-    out_ref[...] = tn(place[...], outq[...]).astype(BF16)
-    leave(0, out_ref, out_to).start()
     g = grad[...]
     high = g.astype(BF16)
     g = g - high.astype(F32)
     mid = g.astype(BF16)
     low = (g - mid.astype(F32)).astype(BF16)
     gfeat_ref[...] = tn(place[...], high) + (tn(place[...], mid) + tn(place[...], low))
-    leave(1, gfeat_ref, gfeat_to).start()
+    leave(4, gfeat_ref, gfeat_to).start()
+    to_sibling(1, 1)
+    out_ref[...] = tn(place[...], outq[...]).astype(BF16)
+    leave(5, out_ref, out_to).start()
+    to_all(0, 1)
     to_sibling(0, 0)
-    to_all(0, 1)
-    finish(1, 0)
-    leave(2, result0.at[1], result0_to.at[1]).start()
-    finish(1, 1)
-    leave(3, result1.at[1], result1_to.at[1]).start()
+    for p in range(2):
+        finish(1, p)
+    for copy in leave_all(1):
+        copy.start()
     for n in range(4):
         halo_done(n)
     to_sibling(0, 1)
-    finish(0, 0)
-    leave(4, result0.at[0], result0_to.at[0]).start()
-    finish(0, 1)
-    leave(5, result1.at[0], result1_to.at[0]).start()
-    leave(0, out_ref, out_to).wait()
-    leave(1, gfeat_ref, gfeat_to).wait()
-    leave(2, result0.at[1], result0_to.at[1]).wait()
-    leave(3, result1.at[1], result1_to.at[1]).wait()
-    leave(4, result0.at[0], result0_to.at[0]).wait()
-    leave(5, result1.at[0], result1_to.at[0]).wait()
+    for p in range(2):
+        finish(0, p)
+    for copy in leave_all(0):
+        copy.start()
+    for copy in leave_all(0) + leave_all(1):
+        copy.wait()
+    leave(4, gfeat_ref, gfeat_to).wait()
+    leave(5, out_ref, out_to).wait()
 
 
 def unpack(out_in, gfeat_in, result0_in, result1_in,
@@ -644,24 +653,24 @@
         t, r = divmod(index, CH // 8)
         ref[l, 8 * r : 8 * r + 8, LANES * t : LANES * t + LANES] = tile
 
+    def place_any(l, index, tile):
+        if index < TILES:
+            place_tile(l, gdown, index, tile)
+        else:
+            place_tile(l, gup, index - TILES, tile)
+
     copies[0].wait()
     for l in range(2):
         for chunk in range(2 * CHUNKS):
             v = result0[l, chunk // CHUNKS, chunk % CHUNKS].astype(F32)
-            for slot in range(4):
-                place_tile(l, gdown, 4 * chunk + slot, v[8 * slot : 8 * slot + 8])
+            for slot in range(8):
+                place_any(l, 8 * chunk + slot, v[8 * slot : 8 * slot + 8])
     copies[1].wait()
     for l in range(2):
         pair = []
         for chunk in range(2 * CHUNKS):
             v = result1[l, chunk // CHUNKS, chunk % CHUNKS].astype(F32)
-            for slot in range(5):
-                index = 5 * chunk + slot
-                tile = v[8 * slot : 8 * slot + 8]
-                if index < CH // 8 * 6:
-                    place_tile(l, gup, index, tile)
-                else:
-                    place_tile(l, gdown, index - CH // 8 * 6 + DTILES, tile)
+            place_any(l, 256 + chunk, v[:8])
             v = v[SMALL_AT:]
             pair.append(v + pltpu.roll(v, 4, 0))
             if chunk % 2:
@@ -718,7 +727,7 @@
             pltpu.VMEM((2, *wide), F32),
             pltpu.VMEM(wide, F32),
             pltpu.VMEM((NI, PACK, NS, LANES), F32),
-            pltpu.VMEM((TC * NS, CH), F32),
+            pltpu.VMEM((NI, TC * NS, CH), F32),
             pltpu.VMEM((2, PX, CH), F32),
             pltpu.VMEM((2, PX, 1), F32),
             pltpu.VMEM((2, PX, CH), BF16),

time: 84.9 us -> 81.8 us (0.963)
  Pallas kernels: 84.1 us -> 80.9 us
    pallas_call x1, Pallas kernels: 80.8 us -> 77.7 us  [on_device(): pl.pallas_call(functools.partial(kernel, 1.0 / math.sqrt(pixel_total)), o...]
where the time goes in v5:
time: 81.8 us; the launch traced here: 81.6 us
  Pallas kernels  80.9 us (99%)
    pallas_call x1, Pallas kernels, on_device(): pl.pallas_call(functools.partial(kernel, 1.0 / math.sqrt(pixel_total)), o...  77.7 us
    pallas_call x1, Pallas kernels, on_device(): pl.pallas_call(unpack, out_shape=(jax.ShapeDtypeStruct((PX, CH), BF16), j...  3.26 us

profile of v5, /device:TPU:1, one launch (start us, length us, event | category | flops | bytes accessed | tf_op | source)
XLA Modules:
  0.0 81.6 jit_solution(10896581052492516864)
XLA Ops:
  0.6 77.7 %shard_map.221 = (bf16[512,192]{1,0:T(8,128)(2,1)}, f32[512,192]{1,0:T(8,128)}, bf16[2,2,16,64,128]{4,3,2,1,0:T(8,128)(2,1)}, bf16[2,2,16,16,128]{4,3,2,1,0:T(8,128)(2,1)}) custom-call(bf16[512,192]{1,0:T(8,128)(2,1)} %bitcast.13, bf16[512,192]{1,0:T(8,128)(2,1)} %bitcast.14, f32[49,2,192]{2,1,0:T(2,128)} %bitcast.15, f32[2,192]{1,0:T(2,128)} %cbias.1, ...), custom_call_target="tpu_custom_call" | custom-call | tf_op jit(solution)/shard_map/pallas_call | solution.py:703
  78.3 3.3 %shard_map.222 = (bf16[512,192]{1,0:T(8,128)(2,1)}, f32[512,192]{1,0:T(8,128)}, f32[49,2,192]{2,1,0:T(2,128)}, f32[2,192]{1,0:T(2,128)}, f32[2,192]{1,0:T(2,128)...) custom-call(bf16[512,192]{1,0:T(8,128)(2,1)} %get-tuple-element.26.o, ...), custom_call_target="tpu_custom_call" | custom-call | tf_op jit(solution)/shard_map/pallas_call | solution.py:771

commit v6 on v5

--- a/solution.py
+++ b/solution.py
@@ -102,29 +102,29 @@
         pz = lax.rem(z + d, NZ)
         return pz, (yh, ty, pz * 4 + yl * 2 + core)
 
-    barrier = pltpu.get_barrier_semaphore()
-
-    def greet(device):
-        pl.semaphore_signal(barrier, inc=1, device_id=device, device_id_type=MESH)
-
-    for dy, dx in HALOS:
-        greet((yh, lax.rem(ty + dy + 4, 4), lax.rem(tx + dx + 32, 32)))
-    greet(sibling)
-
-    @pl.loop(1, CHUNKS)
-    def _(d):
-        greet(plane_peer(d)[1])
-
-    @pl.loop(1, NZ)
-    def _(d):
-        greet(z_peer(d)[1])
-
     arrivals = {}
     loads = ((feat_in, feat), (place_in, place), (edges_in, edges), (cot_in, cot), (dw_in, dw), (spread_in, spread),
              (up_in, up), (down_in, down))
     for k, (src, dst) in enumerate(loads):
         arrivals[id(dst)] = pltpu.make_async_copy(src, dst, ins.at[k])
         arrivals[id(dst)].start()
+
+    barrier = pltpu.get_barrier_semaphore()
+
+    def greet(device):
+        pl.semaphore_signal(barrier, inc=1, device_id=device, device_id_type=MESH)
+
+    for dy, dx in HALOS:
+        greet((yh, lax.rem(ty + dy + 4, 4), lax.rem(tx + dx + 32, 32)))
+    greet(sibling)
+
+    @pl.loop(1, CHUNKS)
+    def _(d):
+        greet(plane_peer(d)[1])
+
+    @pl.loop(1, NZ)
+    def _(d):
+        greet(z_peer(d)[1])
 
     def ready(*refs):
         for ref in refs:
@@ -342,8 +342,9 @@
     def up_grads(l):
         weight_tiles(normed.at[l], gpre, lambda index, tile: put(l, TILES + index, tile))
 
-    def tap_grads(l):
-        for part, (cols, base, first) in enumerate(((TC, 0, 0), (TC // 2, TC + 6, TC))):
+    def tap_grads(l, *parts):
+        for part in parts:
+            cols, base, first = ((TC, 0, 0), (TC // 2, TC + 6, TC))[part]
 
             @pl.loop(0, SPAN)
             def _(j):
@@ -574,38 +575,38 @@
     core_copy(1, 0).start()
     sums = backward(1)
     halo_start(2, gx)
+    tap_grads(1, 1)
     to_plane(1, 0)
-    tap_grads(1)
+    tap_grads(1, 0)
     small_grads(1, early, s_ubias, sums)
     core_copy(1, 1).start()
     halo_wait(2)
     assemble(2, gx, qg)
     to_plane(1, 1)
     convolve(qg, 1, True)
-    to_z(1, 0)
     step_back(1)
     early = branch_grads(0)
     s_ubias = pre_grads(0)
     down_grads(0)
     up_grads(0)
     core_copy(0, 0).start()
+    to_z(1, 0)
     to_z(1, 1)
     sums = backward(0)
     halo_start(3, gx)
+    tap_grads(0, 1)
     to_plane(0, 0)
-    to_all(1, 0)
-    tap_grads(0)
+    tap_grads(0, 0)
     small_grads(0, early, s_ubias, sums)
     core_copy(0, 1).start()
-    to_all(1, 1)
     halo_wait(3)
     assemble(3, gx, qg)
-    to_z(0, 0)
     to_plane(0, 1)
+    to_all(1, 0)
+    to_all(1, 1)
     convolve(qg, 0, True)
     step_back(0)
-    to_sibling(1, 0)
-    to_all(0, 0)
+    to_z(0, 0)
     to_z(0, 1)
     g = grad[...]
     high = g.astype(BF16)
@@ -614,15 +615,17 @@
     low = (g - mid.astype(F32)).astype(BF16)
     gfeat_ref[...] = tn(place[...], high) + (tn(place[...], mid) + tn(place[...], low))
     leave(4, gfeat_ref, gfeat_to).start()
-    to_sibling(1, 1)
     out_ref[...] = tn(place[...], outq[...]).astype(BF16)
     leave(5, out_ref, out_to).start()
+    to_sibling(1, 0)
+    to_sibling(1, 1)
+    to_all(0, 0)
     to_all(0, 1)
-    to_sibling(0, 0)
     for p in range(2):
         finish(1, p)
     for copy in leave_all(1):
         copy.start()
+    to_sibling(0, 0)
     for n in range(4):
         halo_done(n)
     to_sibling(0, 1)
@@ -637,16 +640,17 @@
 
 
 def unpack(out_in, gfeat_in, result0_in, result1_in,
-           out, gfeat, gtaps, gcbias, ggain, gshift, gup, gubias, gdown, gdbias, gscale,
-           few, result0, result1, ins):
+           out_to, gfeat_to, gtaps, gcbias, ggain, gshift, gup_to, gubias, gdown_to, gdbias, gscale,
+           few, result0, result1, gup, gdown, ins, outs):
     copies = [
         pltpu.make_async_copy(src, dst, ins.at[k])
         for k, (src, dst) in enumerate(
-            ((result0_in, result0), (result1_in, result1), (gfeat_in, gfeat), (out_in, out))
+            ((result0_in, result0), (result1_in, result1), (gfeat_in, gfeat_to), (out_in, out_to))
         )
     ]
     for copy in copies:
         copy.start()
+    leaving = [pltpu.make_async_copy(gdown, gdown_to, outs.at[0]), pltpu.make_async_copy(gup, gup_to, outs.at[1])]
     upper = lax.broadcasted_iota(jnp.int32, (8, LANES), 0) < 4
 
     def place_tile(l, ref, index, tile):
@@ -665,13 +669,16 @@
             v = result0[l, chunk // CHUNKS, chunk % CHUNKS].astype(F32)
             for slot in range(8):
                 place_any(l, 8 * chunk + slot, v[8 * slot : 8 * slot + 8])
+    leaving[0].start()
     copies[1].wait()
+    for l in range(2):
+        for chunk in range(2 * CHUNKS):
+            place_any(l, 256 + chunk, result1[l, chunk // CHUNKS, chunk % CHUNKS].astype(F32)[:8])
+    leaving[1].start()
     for l in range(2):
         pair = []
         for chunk in range(2 * CHUNKS):
-            v = result1[l, chunk // CHUNKS, chunk % CHUNKS].astype(F32)
-            place_any(l, 256 + chunk, v[:8])
-            v = v[SMALL_AT:]
+            v = result1[l, chunk // CHUNKS, chunk % CHUNKS].astype(F32)[SMALL_AT:]
             pair.append(v + pltpu.roll(v, 4, 0))
             if chunk % 2:
                 few[4 * chunk - 4 : 4 * chunk + 4] = jnp.where(upper, pair[-2], pair[-1])
@@ -684,8 +691,8 @@
             ref[l : l + 1, LANES:] = few[at + 1 : at + 2, :REST]
         for t in range(6):
             gubias[l : l + 1, LANES * t : LANES * t + LANES] = few[ROW_UBIAS + t : ROW_UBIAS + t + 1]
-    copies[2].wait()
-    copies[3].wait()
+    for copy in copies[2:] + leaving:
+        copy.wait()
 
 
 def on_device(features, cotangent, dw_kernel, conv_bias, ln_gain, ln_shift, up_weight, up_bias,
@@ -777,11 +784,14 @@
             vector, vector, vector, weight, jax.ShapeDtypeStruct((depth, HID), F32), weight, vector, vector,
         ),
         in_specs=[hbm] * 4,
-        out_specs=(vmem,) * 11,
+        out_specs=(hbm,) * 2 + (vmem,) * 4 + (hbm, vmem, hbm) + (vmem,) * 2,
         scratch_shapes=[
             pltpu.VMEM((LANES, LANES), F32),
             *(pltpu.VMEM(v.shape, v.dtype) for v in results),
+            pltpu.VMEM((depth, CH, HID), F32),
+            pltpu.VMEM((depth, CH, HID), F32),
             dma((4,)),
+            dma((2,)),
         ],
         compiler_params=pltpu.CompilerParams(vmem_limit_bytes=56 * 2**20),
     )(out, gfeat, result0, result1)

time: 81.8 us -> 102 us (1.25)
  Pallas kernels: 80.9 us -> 101 us
    pallas_call x1, Pallas kernels: 3.26 us -> 25.6 us  [on_device(): pl.pallas_call(unpack, out_shape=(jax.ShapeDtypeStruct((PX, CH), BF16), j...]
    pallas_call x1, Pallas kernels: 77.7 us -> 75.3 us  [on_device(): pl.pallas_call(functools.partial(kernel, 1.0 / math.sqrt(pixel_total)), o...]
where the time goes in v6:
time: 102 us
  Pallas kernels  101 us (99%)
    pallas_call x1, Pallas kernels, on_device(): pl.pallas_call(functools.partial(kernel, 1.0 / math.sqrt(pixel_total)), o...  75.3 us
    pallas_call x1, Pallas kernels, on_device(): pl.pallas_call(unpack, out_shape=(jax.ShapeDtypeStruct((PX, CH), BF16), j...  25.6 us

profile of v6, /device:TPU:1, one launch (start us, length us, event | category | flops | bytes accessed | tf_op | source)
XLA Modules:
  0.0 101.6 jit_solution(329311999949531144)
XLA Ops:
  0.6 75.3 %shard_map.221 = (bf16[512,192]{1,0:T(8,128)(2,1)}, f32[512,192]{1,0:T(8,128)}, bf16[2,2,16,64,128]{4,3,2,1,0:T(8,128)(2,1)}, bf16[2,2,16,16,128]{4,3,2,1,0:T(8,128)(2,1)}) custom-call(bf16[512,192]{1,0:T(8,128)(2,1)} %bitcast.13, bf16[512,192]{1,0:T(8,128)(2,1)} %bitcast.14, f32[49,2,192]{2,1,0:T(2,128)} %bitcast.15, f32[2,192]{1,0:T(2,128)} %cbias.1, ...), custom_call_target="tpu_custom_call" | custom-call | tf_op jit(solution)/shard_map/pallas_call | solution.py:710
  75.9 25.6 %shard_map.222 = (bf16[512,192]{1,0:T(8,128)(2,1)}, f32[512,192]{1,0:T(8,128)}, f32[49,2,192]{2,1,0:T(2,128)}, f32[2,192]{1,0:T(2,128)}, f32[2,192]{1,0:T(2,128)...) custom-call(bf16[512,192]{1,0:T(8,128)(2,1)} %get-tuple-element.26.o, ...), custom_call_target="tpu_custom_call" | custom-call | tf_op jit(solution)/shard_map/pallas_call | solution.py:778

commit v7 on v6

--- a/solution.py
+++ b/solution.py
@@ -203,7 +203,7 @@
             q[0:3, slot] = jnp.where(row == 0, top, pltpu.roll(mid[1:4], 1, 1))
             q[7:10, slot] = jnp.where(row == NS - 1, low, pltpu.roll(mid[0:3], NS - 1, 1))
 
-        @pl.loop(0, TC + 6)
+        @pl.loop(0, TC + 6, unroll=2)
         def _(cc):
             fill(cc, plane[:, cc, :, :LANES], tq[0, :, cc, :, :LANES], tq[1, :, cc, :, :LANES])
 
@@ -211,7 +211,7 @@
             return jnp.concatenate([ref[(*at[:-1], at[-1], slice(None), slice(LANES, CH))],
                                     ref[(*at[:-1], at[-1] + 8, slice(None), slice(LANES, CH))]], axis=-1)
 
-        @pl.loop(0, TC // 2 + 6)
+        @pl.loop(0, TC // 2 + 6, unroll=2)
         def _(k):
             fill(TC + 6 + k, pair(plane, slice(None), k), pair(tq, 0, slice(None), k), pair(tq, 1, slice(None), k))
 
@@ -640,12 +640,12 @@
 
 
 def unpack(out_in, gfeat_in, result0_in, result1_in,
-           out_to, gfeat_to, gtaps, gcbias, ggain, gshift, gup_to, gubias, gdown_to, gdbias, gscale,
+           out, gfeat, gtaps, gcbias, ggain, gshift, gup_to, gubias, gdown_to, gdbias, gscale,
            few, result0, result1, gup, gdown, ins, outs):
     copies = [
         pltpu.make_async_copy(src, dst, ins.at[k])
         for k, (src, dst) in enumerate(
-            ((result0_in, result0), (result1_in, result1), (gfeat_in, gfeat_to), (out_in, out_to))
+            ((result0_in, result0), (result1_in, result1), (gfeat_in, gfeat), (out_in, out))
         )
     ]
     for copy in copies:
@@ -784,7 +784,7 @@
             vector, vector, vector, weight, jax.ShapeDtypeStruct((depth, HID), F32), weight, vector, vector,
         ),
         in_specs=[hbm] * 4,
-        out_specs=(hbm,) * 2 + (vmem,) * 4 + (hbm, vmem, hbm) + (vmem,) * 2,
+        out_specs=(vmem,) * 6 + (hbm, vmem, hbm) + (vmem,) * 2,
         scratch_shapes=[
             pltpu.VMEM((LANES, LANES), F32),
             *(pltpu.VMEM(v.shape, v.dtype) for v in results),

time: 102 us -> 77.9 us (0.76)
  Pallas kernels: 101 us -> 77.1 us
    pallas_call x1, Pallas kernels: 25.6 us -> 3.68 us  [on_device(): pl.pallas_call(unpack, out_shape=(jax.ShapeDtypeStruct((PX, CH), BF16), j...]
    pallas_call x1, Pallas kernels: 75.3 us -> 73.4 us  [on_device(): pl.pallas_call(functools.partial(kernel, 1.0 / math.sqrt(pixel_total)), o...]
where the time goes in v7:
time: 77.9 us; the launch traced here: 77.8 us
  Pallas kernels  77.1 us (99%)
    pallas_call x1, Pallas kernels, on_device(): pl.pallas_call(functools.partial(kernel, 1.0 / math.sqrt(pixel_total)), o...  73.4 us
    pallas_call x1, Pallas kernels, on_device(): pl.pallas_call(unpack, out_shape=(jax.ShapeDtypeStruct((PX, CH), BF16), j...  3.68 us

profile of v7, /device:TPU:1, one launch (start us, length us, event | category | flops | bytes accessed | tf_op | source)
XLA Modules:
  0.0 77.8 jit_solution(4097075393036826792)
XLA Ops:
  0.6 73.4 %shard_map.221 = (bf16[512,192]{1,0:T(8,128)(2,1)}, f32[512,192]{1,0:T(8,128)}, bf16[2,2,16,64,128]{4,3,2,1,0:T(8,128)(2,1)}, bf16[2,2,16,16,128]{4,3,2,1,0:T(8,128)(2,1)}) custom-call(bf16[512,192]{1,0:T(8,128)(2,1)} %bitcast.13, bf16[512,192]{1,0:T(8,128)(2,1)} %bitcast.14, f32[49,2,192]{2,1,0:T(2,128)} %bitcast.15, f32[2,192]{1,0:T(2,128)} %cbias.1, ...), custom_call_target="tpu_custom_call" | custom-call | tf_op jit(solution)/shard_map/pallas_call | solution.py:710
  74.1 3.7 %shard_map.222 = (bf16[512,192]{1,0:T(8,128)(2,1)}, f32[512,192]{1,0:T(8,128)}, f32[49,2,192]{2,1,0:T(2,128)}, f32[2,192]{1,0:T(2,128)}, f32[2,192]{1,0:T(2,128)...) custom-call(bf16[512,192]{1,0:T(8,128)(2,1)} %get-tuple-element.26.o, ...), custom_call_target="tpu_custom_call" | custom-call | tf_op jit(solution)/shard_map/pallas_call | solution.py:778

commit v8 on v7

--- a/solution.py
+++ b/solution.py
@@ -361,7 +361,7 @@
                     return tuple(sums)
 
                 zero = jnp.zeros((NS, LANES), F32)
-                sums = lax.fori_loop(0, cols // 2, body, (zero,) * SPAN)
+                sums = lax.fori_loop(0, cols // 2, body, (zero,) * SPAN, unroll=2)
                 for r in range(SPAN):
                     taps[part, r * SPAN + j] = sums[r]
 
@@ -640,8 +640,8 @@
 
 
 def unpack(out_in, gfeat_in, result0_in, result1_in,
-           out, gfeat, gtaps, gcbias, ggain, gshift, gup_to, gubias, gdown_to, gdbias, gscale,
-           few, result0, result1, gup, gdown, ins, outs):
+           out, gfeat, gtaps, gcbias, ggain, gshift, gup, gubias, gdown, gdbias, gscale,
+           few, result0, result1, ins):
     copies = [
         pltpu.make_async_copy(src, dst, ins.at[k])
         for k, (src, dst) in enumerate(
@@ -650,7 +650,6 @@
     ]
     for copy in copies:
         copy.start()
-    leaving = [pltpu.make_async_copy(gdown, gdown_to, outs.at[0]), pltpu.make_async_copy(gup, gup_to, outs.at[1])]
     upper = lax.broadcasted_iota(jnp.int32, (8, LANES), 0) < 4
 
     def place_tile(l, ref, index, tile):
@@ -669,12 +668,10 @@
             v = result0[l, chunk // CHUNKS, chunk % CHUNKS].astype(F32)
             for slot in range(8):
                 place_any(l, 8 * chunk + slot, v[8 * slot : 8 * slot + 8])
-    leaving[0].start()
     copies[1].wait()
     for l in range(2):
         for chunk in range(2 * CHUNKS):
             place_any(l, 256 + chunk, result1[l, chunk // CHUNKS, chunk % CHUNKS].astype(F32)[:8])
-    leaving[1].start()
     for l in range(2):
         pair = []
         for chunk in range(2 * CHUNKS):
@@ -691,7 +688,7 @@
             ref[l : l + 1, LANES:] = few[at + 1 : at + 2, :REST]
         for t in range(6):
             gubias[l : l + 1, LANES * t : LANES * t + LANES] = few[ROW_UBIAS + t : ROW_UBIAS + t + 1]
-    for copy in copies[2:] + leaving:
+    for copy in copies[2:]:
         copy.wait()
 
 
@@ -784,14 +781,11 @@
             vector, vector, vector, weight, jax.ShapeDtypeStruct((depth, HID), F32), weight, vector, vector,
         ),
         in_specs=[hbm] * 4,
-        out_specs=(vmem,) * 6 + (hbm, vmem, hbm) + (vmem,) * 2,
+        out_specs=(vmem,) * 11,
         scratch_shapes=[
             pltpu.VMEM((LANES, LANES), F32),
             *(pltpu.VMEM(v.shape, v.dtype) for v in results),
-            pltpu.VMEM((depth, CH, HID), F32),
-            pltpu.VMEM((depth, CH, HID), F32),
             dma((4,)),
-            dma((2,)),
         ],
         compiler_params=pltpu.CompilerParams(vmem_limit_bytes=56 * 2**20),
     )(out, gfeat, result0, result1)

time: 77.9 us -> 77.3 us (level)
  no operation moved by 1% of the time
where the time goes in v8:
time: 77.3 us; the launch traced here: 77.2 us
  Pallas kernels  76.5 us (99%)
    pallas_call x1, Pallas kernels, on_device(): pl.pallas_call(functools.partial(kernel, 1.0 / math.sqrt(pixel_total)), o...  73.2 us
    pallas_call x1, Pallas kernels, on_device(): pl.pallas_call(unpack, out_shape=(jax.ShapeDtypeStruct((PX, CH), BF16), j...  3.26 us

profile of v8, /device:TPU:1, one launch (start us, length us, event | category | flops | bytes accessed | tf_op | source)
XLA Modules:
  0.0 77.2 jit_solution(12746596985491386400)
XLA Ops:
  0.6 73.2 %shard_map.221 = (bf16[512,192]{1,0:T(8,128)(2,1)}, f32[512,192]{1,0:T(8,128)}, bf16[2,2,16,64,128]{4,3,2,1,0:T(8,128)(2,1)}, bf16[2,2,16,16,128]{4,3,2,1,0:T(8,128)(2,1)}) custom-call(bf16[512,192]{1,0:T(8,128)(2,1)} %bitcast.13, bf16[512,192]{1,0:T(8,128)(2,1)} %bitcast.14, f32[49,2,192]{2,1,0:T(2,128)} %bitcast.15, f32[2,192]{1,0:T(2,128)} %cbias.1, ...), custom_call_target="tpu_custom_call" | custom-call | tf_op jit(solution)/shard_map/pallas_call | solution.py:707
  73.9 3.3 %shard_map.222 = (bf16[512,192]{1,0:T(8,128)(2,1)}, f32[512,192]{1,0:T(8,128)}, f32[49,2,192]{2,1,0:T(2,128)}, f32[2,192]{1,0:T(2,128)}, f32[2,192]{1,0:T(2,128)...) custom-call(bf16[512,192]{1,0:T(8,128)(2,1)} %get-tuple-element.26.o, ...), custom_call_target="tpu_custom_call" | custom-call | tf_op jit(solution)/shard_map/pallas_call | solution.py:775
